TPU v7x, 256 devices: a whole 4x4x8 slice. The times are simulated.
256 devices in a mesh: dp: 32 (over x, z), mp: 8 (over y, core).
Axes of the slice: x: 4, y: 4, z: 8, core: 2. Of those that a mesh axis runs over, the one named last changes fastest.
Arguments:
- vision: bfloat16 [8192, 3200], P(('dp', 'mp')), may hold values from -6 to 6
- vision_gain: float32 [3200], replicated, may hold values from 0.1 to 1.9
- image_slot: int32 [32], replicated, may hold values from 0 to 63, as said below
- text_embed: bfloat16 [16384, 8192], P('dp', 'mp'), may hold values from -6 to 6
- w_proj: bfloat16 [3200, 8192], P(None, 'mp'), may hold values from -0.109375 to 0.109375
- llm_gain: float32 [8192], P('mp'), may hold values from 0.1 to 1.9
- w_key: bfloat16 [8192, 1024], P('mp'), may hold values from -0.0625 to 0.0625
- w_value: bfloat16 [8192, 1024], P('mp'), may hold values from -0.0625 to 0.0625
- key_grad: bfloat16 [16384, 1024], P('dp', 'mp'), may hold values from -6 to 6
- value_grad: bfloat16 [16384, 1024], P('dp', 'mp'), may hold values from -6 to 6
Outputs:
- key_out: bfloat16 [16384, 1024], P('dp', 'mp')
- value_out: bfloat16 [16384, 1024], P('dp', 'mp')
- text_grad: bfloat16 [16384, 8192], P('dp', 'mp')
- vision_grad: bfloat16 [8192, 3200], P(('dp', 'mp'))
Inputs may be any that keep to these rules, and one draw needn't show every extreme that they name: `image_slot`: the 32 entries are different slots. Image i is encoded on index i of dp; slot j covers positions j * 256 to (j + 1) * 256 - 1, so it lies on index j // 2 of dp. One index of dp receives 2 images, every other one at most one.
All inputs are finite; a program needn't handle non-finite values.
Results may differ from a plain program's by a relative error of at most 0.0058.
Values may be sent and summed in bfloat16 or wider, within the bound.
No kernel may reach another device: no remote copies, remote signals or barrier semaphores. Data moves between devices by JAX's collectives and lax.ppermute only.
A program may use at most 128 MiB of HBM per device.

v0:
```python
import jax
import jax.numpy as jnp
from jax import lax
from jax.experimental import pallas as pl
from jax.experimental.pallas import tpu as pltpu
from jax.sharding import PartitionSpec as P

D = 8192
DV = 3200
PATCH = 256
LANE = 128
CHUNK = 16
BF = jnp.bfloat16
F32 = jnp.float32
VMEM = pl.BlockSpec(memory_space=pltpu.VMEM)
SMEM = pl.BlockSpec(memory_space=pltpu.SMEM)
HBM = pl.BlockSpec(memory_space=pltpu.HBM)
ANY = pl.BlockSpec(memory_space=pl.ANY)
DMA = pltpu.SemaphoreType.DMA

RING = 4
UP = [(2 * y + c, 2 * ((y + 1) % RING) + c) for y in range(RING) for c in range(2)]
DOWN = [(2 * y + c, 2 * ((y + 3) % RING) + c) for y in range(RING) for c in range(2)]
ACROSS = [(2 * y + c, 2 * ((y + 2) % RING) + c) for y in range(RING) for c in range(2)]
SPLIT = [(2 * y + c, 2 * ((y + 1 + 2 * c) % RING) + c) for y in range(RING) for c in range(2)]
PEER = [(2 * y + c, 2 * y + 1 - c) for y in range(RING) for c in range(2)]


def up(x):
    return lax.ppermute(x, "mp", UP)


def down(x):
    return lax.ppermute(x, "mp", DOWN)


def across(x):
    return lax.ppermute(x, "mp", ACROSS)


def peer(x):
    return lax.ppermute(x, "mp", PEER)


TOKEN = jax.ShapeDtypeStruct((8, LANE), F32)


def call(kernel, name, outs, args, scalars=0, far=(), far_outs=(), scratch=(), flops=0, after=(), token=False):
    size = sum(a.size * a.dtype.itemsize for a in args) + sum(o.size * o.dtype.itemsize for o in outs)
    args, outs = list(args), list(outs)
    ins, results = len(args), len(outs)

    def body(*refs):
        mine = refs[:ins] + refs[ins + len(after) : ins + len(after) + results]
        rest = refs[ins + len(after) + results :]
        if token:
            rest[0][...] = jnp.zeros(TOKEN.shape, F32)
            rest = rest[1:]
        kernel(*mine, *rest)

    return pl.pallas_call(
        body,
        in_specs=[SMEM if i < scalars else HBM if i in far else VMEM for i in range(ins)] + [ANY] * len(after),
        out_specs=[HBM if i in far_outs else VMEM for i in range(results)] + [VMEM] * token,
        out_shape=outs + [TOKEN] * token,
        scratch_shapes=list(scratch),
        compiler_params=pltpu.CompilerParams(vmem_limit_bytes=(52 if far else 8) * 1024 * 1024),
        cost_estimate=pl.CostEstimate(flops=flops, bytes_accessed=size, transcendentals=0),
        name=name,
    )(*args, *after)


def shape(dims, dtype):
    return jax.ShapeDtypeStruct(dims, dtype)


def dot(a, b):
    return jnp.dot(a, b, preferred_element_type=F32)


def dot_t(a, b):
    return lax.dot_general(a, b, (((1,), (1,)), ((), ())), preferred_element_type=F32)


def as_row(column):
    n = column.shape[0]
    return jnp.transpose(jnp.broadcast_to(column, (n, LANE)))[:1]


def as_column(row):
    n = row.shape[1]
    return jnp.transpose(jnp.broadcast_to(row, (LANE, n)))[:, :1]


def lane_block(ref, index, rows=slice(None)):
    return ref[rows, pl.ds(pl.multiple_of(index * LANE, LANE), LANE)]


def vision_norm(vision, gain):
    def kernel(v_ref, g_ref, o_ref, s_ref):
        v = v_ref[...].astype(F32)
        scale = lax.rsqrt(jnp.mean(v * v, axis=1, keepdims=True) + 1e-06)
        s_ref[...] = scale
        o_ref[...] = (v * scale * g_ref[...]).astype(BF)

    rows = vision.shape[0]
    return call(
        kernel, "vision_norm", [shape(vision.shape, BF), shape((rows, 1), F32)], [vision, gain], token=True
    )


def pack_grads(key_grad, value_grad, after):
    rows = key_grad.shape[0]
    slots = rows // PATCH
    per = PATCH // CHUNK
    grads = [g.reshape(slots, per, CHUNK, LANE) for g in (key_grad, value_grad)]

    def kernel(k_ref, v_ref, stack_ref, chunk_ref, sems):
        pairs = []
        for j, ref in enumerate((k_ref, v_ref)):
            for s in range(slots):
                pairs.append((ref.at[s], chunk_ref.at[pl.ds(j * per, per), s]))
            pairs.append((ref, stack_ref.at[j]))
        for wait in load_all(pairs, sems):
            wait()

    stack, chunks, token = call(
        kernel,
        "pack_grads",
        [shape((2, slots, per, CHUNK, LANE), BF), shape((2 * per, slots, CHUNK, LANE), BF)],
        grads,
        far=(0, 1),
        far_outs=(0, 1),
        scratch=[DMA((2 * slots + 2,))],
        after=after,
        token=True,
    )
    return stack.reshape(2 * rows, LANE), chunks, token


def take_blocks(index, x, after):
    count = index.shape[0]

    def kernel(index_ref, x_ref, o_ref):
        for j in range(count):
            o_ref[j] = x_ref[index_ref[j]]

    return call(kernel, "take_blocks", [shape((count,) + x.shape[1:], x.dtype)], [index, x], scalars=1, after=after, token=True)


def load_all(pairs, sems):
    copies = [pltpu.make_async_copy(src, dst, sems.at[i]) for i, (src, dst) in enumerate(pairs)]
    for copy in copies:
        copy.start()
    return [copy.wait for copy in copies]


def text_forward(text, gain, w_key, w_value, after):
    rows, width = text.shape
    blocks = w_key.shape[1] // LANE

    def kernel(t_far, g_ref, k_far, v_far, o_ref, q_ref, t_ref, k_ref, v_ref, scaled, sems):
        waits = load_all([(t_far, t_ref), (k_far, k_ref), (v_far, v_ref)], sems)
        waits[0]()

        @pl.loop(0, rows // LANE)
        def _(i):
            at = pl.ds(pl.multiple_of(i * LANE, LANE), LANE)
            t = t_ref[at].astype(F32)
            scaled[at] = (t * g_ref[...]).astype(BF)
            q_ref[pl.ds(i, 1)] = as_row(jnp.sum(t * t, axis=1, keepdims=True))

        waits[1]()
        waits[2]()

        @pl.loop(0, blocks)
        def _(b):
            w = jnp.concatenate([lane_block(k_ref, b), lane_block(v_ref, b)], axis=1)
            o_ref[b] = dot(scaled[...], w).astype(BF)

    return call(
        kernel,
        "text_forward",
        [shape((blocks, rows, 2 * LANE), BF), shape((rows // LANE, LANE), F32)],
        [text, gain, w_key, w_value],
        far=(0, 2, 3),
        after=after,
        token=True,
        scratch=[
            pltpu.VMEM(text.shape, BF),
            pltpu.VMEM(w_key.shape, BF),
            pltpu.VMEM(w_value.shape, BF),
            pltpu.VMEM((rows, width), BF),
            DMA((3,)),
        ],
        flops=4 * rows * width * w_key.shape[1],
    )


def image_forward(where, order, pieces, w_proj, gain, w_key, w_value, after):
    rows_each = PATCH // 8
    depth, width = w_proj.shape

    def kernel(where_ref, order_ref, *refs):
        piece_refs = refs[: len(pieces)]
        p_far, g_ref, k_far, v_far, e_ref, far_ref, near_ref, q_ref, p_ref, k_ref, v_ref, vis, scaled, sems = refs[
            len(pieces) :
        ]
        cuts = [slice(n * 256, (n + 1) * 256) for n in range(width // 256)]
        waits = load_all(
            [(p_far.at[:, at], p_ref.at[n]) for n, at in enumerate(cuts)] + [(k_far, k_ref), (v_far, v_ref)], sems
        )
        b = 0
        for ref in piece_refs:
            vis[pl.ds(pl.multiple_of(where_ref[b] * rows_each, rows_each), ref.shape[0])] = ref[...]
            b += ref.shape[0] // rows_each

        for n, at in enumerate(cuts):
            waits[n]()
            e_ref[:, at] = dot(vis[...], p_ref[n]).astype(BF)

        @pl.loop(0, PATCH // LANE)
        def _(i):
            at = pl.ds(pl.multiple_of(i * LANE, LANE), LANE)
            e = e_ref[at].astype(F32)
            scaled[at] = (e * g_ref[...]).astype(BF)
            q_ref[pl.ds(i, 1)] = as_row(jnp.sum(e * e, axis=1, keepdims=True))

        waits[-2]()
        waits[-1]()

        @pl.loop(0, RING)
        def _(b):
            there = order_ref[RING + b]
            w = jnp.concatenate([lane_block(k_ref, there), lane_block(v_ref, there)], axis=1)
            far_ref[b] = dot(scaled[...], w).astype(BF)
            own = order_ref[b]
            w = jnp.concatenate([lane_block(k_ref, own), lane_block(v_ref, own)], axis=1)
            near_ref[b] = dot(scaled[...], w)

    return call(
        kernel,
        "image_forward",
        [
            shape((PATCH, width), BF),
            shape((RING, PATCH, 2 * LANE), BF),
            shape((RING, PATCH, 2 * LANE), F32),
            shape((PATCH // LANE, LANE), F32),
        ],
        [where, order, *pieces, w_proj, gain, w_key, w_value],
        scalars=2,
        token=True,
        far=(2 + len(pieces), 4 + len(pieces), 5 + len(pieces)),
        scratch=[
            pltpu.VMEM((width // 256, depth, 256), BF),
            pltpu.VMEM(w_key.shape, BF),
            pltpu.VMEM(w_value.shape, BF),
            pltpu.VMEM((PATCH, depth), BF),
            pltpu.VMEM((PATCH, width), BF),
            DMA((width // 256 + 2,)),
        ],
        flops=2 * PATCH * width * (depth + 2 * w_key.shape[1]),
        after=after,
    )


def backward(order, pieces, w_key, w_value, gain, embed, after):
    rows, width = embed.shape
    cols = w_key.shape[1]
    cuts = width // 256

    def kernel(order_ref, *refs):
        piece_refs = refs[: len(pieces)]
        k_far, v_far, g_ref, e_far, d_out, i_ref, k_ref, v_ref, e_ref, gk, gv, sems, d_held, out_sems = refs[len(pieces) :]
        d_ref = d_held if rows > PATCH else d_out
        outgoing = []
        pairs = []
        b = 0
        for ref in piece_refs:
            for j in range(ref.shape[0] // (2 * rows)):
                at = pl.ds(pl.multiple_of(order_ref[b] * LANE, LANE), LANE)
                pairs.append((ref.at[pl.ds(2 * rows * j, rows)], gk.at[:, at]))
                pairs.append((ref.at[pl.ds(2 * rows * j + rows, rows)], gv.at[:, at]))
                b += 1
        for n in range(cuts):
            at = pl.ds(n * 256, 256)
            pairs += [(k_far.at[at], k_ref.at[at]), (v_far.at[at], v_ref.at[at])]
        pairs.append((e_far, e_ref))
        waits = load_all(pairs, sems)
        for wait in waits[:16]:
            wait()
        for n in range(cuts):
            at = slice(n * 256, (n + 1) * 256)
            waits[16 + 2 * n]()
            waits[17 + 2 * n]()
            d = dot_t(gk[...], k_ref[at]) + dot_t(gv[...], v_ref[at])
            d_ref[:, at] = d * g_ref[:, at]
            if rows > PATCH:
                outgoing.append(pltpu.make_async_copy(d_ref.at[:, at], d_out.at[:, at], out_sems.at[n]))
                outgoing[-1].start()
        waits[-1]()

        @pl.loop(0, rows // LANE)
        def _(i):
            at = pl.ds(pl.multiple_of(i * LANE, LANE), LANE)
            i_ref[pl.ds(i, 1)] = as_row(jnp.sum(d_ref[at] * e_ref[at].astype(F32), axis=1, keepdims=True))

        for copy in outgoing:
            copy.wait()

    n = len(pieces)
    return call(
        kernel,
        "backward",
        [shape((rows, width), F32), shape((rows // LANE, LANE), F32)],
        [order, *pieces, w_key, w_value, gain, embed],
        scalars=1,
        far=tuple(range(1, n + 3)) + (n + 4,),
        scratch=[
            pltpu.VMEM(w_key.shape, BF),
            pltpu.VMEM(w_value.shape, BF),
            pltpu.VMEM(embed.shape, BF),
            pltpu.VMEM((rows, cols), BF),
            pltpu.VMEM((rows, cols), BF),
            DMA((17 + 2 * cuts,)),
            pltpu.VMEM(embed.shape if rows > PATCH else (8, LANE), F32),
            DMA((cuts,)),
        ],
        flops=4 * rows * width * cols,
        after=after,
        far_outs=(0,) if rows > PATCH else (),
        token=True,
    )


def embed_grad(d, e, square_row, inner_row):
    scale = lax.rsqrt(as_column(square_row) / D + 1e-05)
    inner = as_column(inner_row) / D
    return scale * d - e * (scale * scale * scale * inner)


def image_backward(order, image_d, embed, square, inner, w_proj, after):
    depth, width = w_proj.shape
    rows_each = PATCH // 8
    half = PATCH // 2
    cut = 640

    def kernel(order_ref, d_ref, e_ref, q_ref, i_ref, p_far, far_ref, near_ref, p_ref, grad, turned, sems):
        cuts = [slice(n * cut, (n + 1) * cut) for n in range(depth // cut)]
        waits = load_all([(p_far.at[at], p_ref.at[at]) for at in cuts], sems)

        @pl.loop(0, PATCH // LANE)
        def _(i):
            at = pl.ds(pl.multiple_of(i * LANE, LANE), LANE)
            row = pl.ds(i, 1)
            grad[at] = embed_grad(d_ref[at], e_ref[at].astype(F32), q_ref[row], i_ref[row]).astype(BF)

        for b in range(8):
            at = pl.ds(pl.multiple_of(order_ref[b] * rows_each, rows_each), rows_each)
            turned[b * rows_each : (b + 1) * rows_each] = grad[at]

        for n, at in enumerate(cuts):
            waits[n]()
            r = dot_t(turned[...], p_ref[at])
            near_ref[:, at] = r[:half]
            far_ref[:, at] = r[half:].astype(BF)

    return call(
        kernel,
        "image_backward",
        [shape((half, depth), BF), shape((half, depth), F32)],
        [order, image_d, embed, square, inner, w_proj],
        scalars=1,
        far=(5,),
        scratch=[
            pltpu.VMEM(w_proj.shape, BF),
            pltpu.VMEM((PATCH, width), BF),
            pltpu.VMEM((PATCH, width), BF),
            DMA((depth // cut,)),
        ],
        flops=2 * PATCH * width * depth,
        after=after,
        token=True,
    )


def ring_first(near, other, after):
    _, n, c = near.shape
    h = n // 2

    def kernel(a_ref, b_ref, up_ref, down_ref, here_ref, above_ref, below_ref):
        def total(k, at):
            return a_ref[k, at] + b_ref[k, at].astype(F32)

        first, second = slice(0, h), slice(h, n)
        up_ref[first] = total(2, first).astype(BF)
        up_ref[second] = total(1, second).astype(BF)
        down_ref[first] = total(3, first).astype(BF)
        down_ref[second] = total(2, second).astype(BF)
        here_ref[...] = total(0, slice(0, n))
        above_ref[...] = total(1, first)
        below_ref[...] = total(3, second)

    return call(
        kernel,
        "ring_first",
        [shape((n, c), BF), shape((n, c), BF), shape((n, c), F32), shape((h, c), F32), shape((h, c), F32)],
        [near, other],
        after=after,
        token=True,
    )


def ring_sum(near, far, after=()):
    up1, down1, here, above, below, token = ring_first(near, peer(far).reshape(near.shape), after)
    h = above.shape[0]
    up1, down1 = up(up1), down(down1)
    up2 = up((above + up1[:h].astype(F32)).astype(BF))
    down2 = down((below + down1[h:].astype(F32)).astype(BF))
    return (here, up1, down1, up2, down2), token


def ring_total(here_ref, up1_ref, down1_ref, up2_ref, down2_ref):
    h = up2_ref.shape[0]
    first = here_ref[:h] + down1_ref[:h].astype(F32) + up2_ref[...].astype(F32)
    second = here_ref[h:] + up1_ref[h:].astype(F32) + down2_ref[...].astype(F32)
    return first, second


def image_out(pieces, square, after):
    h = PATCH // 2

    def kernel(*refs):
        q_ref, o_ref = refs[5:7]
        for j, t in enumerate(ring_total(*refs[:5])):
            scale = lax.rsqrt(as_column(q_ref[j : j + 1]) / D + 1e-05)
            t = (t * scale).astype(BF)
            o_ref[j * h : (j + 1) * h] = t[:, :LANE]
            o_ref[PATCH + j * h : PATCH + (j + 1) * h] = t[:, LANE:]

    return call(kernel, "image_out", [shape((2 * PATCH, LANE), BF)], [*pieces, square], after=after, token=True)


def vision_out(pieces, vision, gain, scale):
    rows = vision.shape[0]
    h = rows // 2

    def kernel(*refs):
        v_ref, g_ref, s_ref, o_ref = refs[5:]
        for j, t in enumerate(ring_total(*refs[:5])):
            at = slice(j * h, (j + 1) * h)
            v, s = v_ref[at].astype(F32), s_ref[at]
            grad_h = t.astype(BF).astype(F32) * g_ref[...]
            inner = jnp.mean(grad_h * v, axis=1, keepdims=True)
            o_ref[at] = (s * grad_h - v * (s * s * s * inner)).astype(BF)

    return call(kernel, "vision_out", [shape(vision.shape, BF)], [*pieces, vision, gain, scale])[0]


def text_out(filled, text_d, text, square, inner, after):
    rows, width = text.shape
    parts = rows // LANE

    def kernel(f_ref, d_far, t_far, q_ref, i_ref, o_far, d_ref, t_ref, o_ref, sems, out_sems):
        cuts = [pl.ds(i * LANE, LANE) for i in range(parts)]
        waits = load_all([(d_far.at[at], d_ref.at[at]) for at in cuts] + [(t_far.at[at], t_ref.at[at]) for at in cuts], sems)
        outgoing = []
        for i, at in enumerate(cuts):
            waits[i]()
            waits[parts + i]()
            row = pl.ds(i, 1)
            grad = embed_grad(d_ref[at], t_ref[at].astype(F32), q_ref[row], i_ref[row])
            o_ref[at] = jnp.where(f_ref[i // (PATCH // LANE)] > 0, 0.0, grad).astype(BF)
            outgoing.append(pltpu.make_async_copy(o_ref.at[at], o_far.at[at], out_sems.at[i]))
            outgoing[-1].start()
        for copy in outgoing:
            copy.wait()

    return call(
        kernel,
        "text_out",
        [shape((rows, width), BF)],
        [filled, text_d, text, square, inner],
        scalars=1,
        far=(1, 2),
        far_outs=(0,),
        scratch=[
            pltpu.VMEM(text.shape, F32),
            pltpu.VMEM(text.shape, BF),
            pltpu.VMEM(text.shape, BF),
            DMA((2 * parts,)),
            DMA((parts,)),
        ],
        after=after,
        token=True,
    )


def key_value_out(filled, text_kv, square, arrived):
    rows = text_kv.shape[0]
    per = PATCH // CHUNK

    def kernel(f_ref, t_ref, q_ref, a_ref, k_ref, v_ref):
        for s in range(rows // PATCH):
            @pl.when(f_ref[s] > 0)
            def _():
                for c in range(per):
                    at = pl.ds(s * PATCH + c * CHUNK, CHUNK)
                    k_ref[at] = a_ref[c, s]
                    v_ref[at] = a_ref[per + c, s]

            @pl.when(f_ref[s] == 0)
            def _():
                for i in range(PATCH // LANE):
                    j = s * (PATCH // LANE) + i
                    at = pl.ds(j * LANE, LANE)
                    scale = lax.rsqrt(as_column(q_ref[j : j + 1]) / D + 1e-05)
                    t = (t_ref[at].astype(F32) * scale).astype(BF)
                    k_ref[at] = t[:, :LANE]
                    v_ref[at] = t[:, LANE:]

    return call(
        kernel,
        "key_value_out",
        [shape((rows, LANE), BF), shape((rows, LANE), BF)],
        [filled, text_kv, square, arrived],
        scalars=1,
    )


def join(core, x, other):
    rows = x.shape[0]

    def kernel(c_ref, x_ref, other_ref, o_ref):
        for c in range(2):
            @pl.when(c_ref[0] == c)
            def _():
                o_ref[c * rows : (c + 1) * rows] = x_ref[...]
                o_ref[(1 - c) * rows : (2 - c) * rows] = other_ref[...]

    return call(kernel, "join", [shape((2 * rows,) + x.shape[1:], x.dtype)], [core, x, other], scalars=1)[0]


def chip_gather(core, x):
    rows = x.shape[0]
    block = join(core, x, peer(x))
    near = lax.ppermute(block, "mp", SPLIT)
    far = lax.ppermute(lax.dynamic_slice_in_dim(near, core[0] * rows, rows), "mp", SPLIT)
    return [block, near, peer(near), far, peer(far)]


def small_sum(x):
    pair = x + peer(x)
    pair = pair + up(pair)
    return pair + across(pair)


def shards(
    vision,
    vision_gain,
    image_slot,
    text_embed,
    w_proj,
    llm_gain,
    w_key,
    w_value,
    key_grad,
    value_grad,
):
    dp = lax.axis_size("dp")
    here = lax.axis_index("dp")
    m = lax.axis_index("mp")
    y, c = m // 2, m % 2
    slots = text_embed.shape[0] // PATCH
    text_rows = text_embed.shape[0] // LANE

    rel = jnp.arange(8, dtype=jnp.int32)
    order = ((y + rel % RING) % RING) * 2 + (c ^ (rel // RING))
    core = c[None]
    near, next_, far = (y + 3 + 2 * c) % RING, (y + 1 + 2 * c) % RING, (y + 2) % RING
    where = jnp.stack(
        [2 * y, 2 * y + 1, 2 * near, 2 * near + 1, 2 * next_, 2 * next_ + 1, 2 * far + c, 2 * far + 1 - c]
    )
    slot_ids = jnp.arange(dp * slots, dtype=jnp.int32)
    onehot = slot_ids[:, None] == image_slot[None, :]
    owner = jnp.sum(jnp.where(onehot, jnp.arange(dp, dtype=jnp.int32)[None, :], 0), axis=1)
    mine = slot_ids[:slots] + here * slots
    filled = jnp.any(mine[:, None] == image_slot[None, :], axis=1).astype(jnp.int32)
    gain = llm_gain[None]
    vis_gain = vision_gain[None]

    vis_normed, vis_scale, norm_done = vision_norm(vision, vis_gain)
    with jax.named_scope("vision_gather"):
        vis_parts = chip_gather(core, vis_normed)

    grad_stack, grad_chunks, packed_done = pack_grads(key_grad, value_grad, [norm_done])
    with jax.named_scope("slot_grads_spread"):
        spread = lax.all_to_all(grad_chunks, "dp", split_axis=0, concat_axis=0, tiled=True)
    with jax.named_scope("text_grad_gather"):
        text_g = lax.all_gather(grad_stack, "mp", axis=0, tiled=True)
    picked, picked_done = take_blocks(
        image_slot, spread.reshape(dp * slots, CHUNK, LANE), [packed_done, vis_parts[3]]
    )
    with jax.named_scope("slot_grads_collect"):
        image_kv_grad = lax.all_to_all(picked, "dp", split_axis=0, concat_axis=0, tiled=True)

    embed, far, near, image_square, image_done = image_forward(
        where, order, vis_parts, w_proj, gain, w_key, w_value, [picked_done]
    )
    text_part, text_square, text_done = text_forward(text_embed, gain, w_key, w_value, [image_done])
    with jax.named_scope("text_key_value_sum"):
        text_kv = lax.psum_scatter(text_part, "mp", scatter_dimension=0, tiled=False)
    with jax.named_scope("image_key_value_sum"):
        pieces, kv_ring = ring_sum(near, far, [text_done, image_kv_grad])
    with jax.named_scope("image_grad_gather"):
        image_g = chip_gather(core, image_kv_grad.reshape(2 * PATCH, LANE))
    with jax.named_scope("squares_sum"):
        squares = small_sum(jnp.concatenate([text_square, image_square]))
    text_square, image_square = squares[:text_rows], squares[text_rows:]

    image_kv, kv_out = image_out(pieces, image_square, ())
    with jax.named_scope("image_out_spread"):
        spread = lax.all_to_all(
            image_kv.reshape(dp, CHUNK, LANE), "dp", split_axis=0, concat_axis=0, tiled=True
        )

    text_d, text_inner, text_back = backward(
        rel, [text_g], w_key, w_value, gain, text_embed, [kv_ring, pieces[1], pieces[2]]
    )
    image_d, image_inner, _ = backward(where, image_g, w_key, w_value, gain, embed, [text_back, kv_out])
    with jax.named_scope("inner_sum"):
        inner = small_sum(jnp.concatenate([text_inner, image_inner]))
    d_far, d_near, back_done = image_backward(
        order, image_d, embed, image_square, inner[text_rows:], w_proj, [spread]
    )
    with jax.named_scope("d_vis_sum"):
        d_pieces, d_ring = ring_sum(d_near.reshape(RING, -1, DV), d_far)
    packed, _ = take_blocks(owner, spread, [d_ring])
    with jax.named_scope("image_out_collect"):
        arrived = lax.all_to_all(
            packed.reshape(dp, slots, CHUNK, LANE), "dp", split_axis=0, concat_axis=0, tiled=True
        )
    text_grad, _ = text_out(
        filled, text_d, text_embed, text_square, inner[:text_rows], [back_done, *d_pieces[1:3]]
    )
    key_out, value_out = key_value_out(filled, text_kv, text_square, arrived)
    vision_grad = vision_out(d_pieces, vision, vis_gain, vis_scale)
    return key_out, value_out, text_grad, vision_grad


def solution(mesh):
    placed = (
        P(("dp", "mp"), None),
        P(),
        P(),
        P("dp", "mp"),
        P(None, "mp"),
        P("mp"),
        P("mp", None),
        P("mp", None),
        P("dp", "mp"),
        P("dp", "mp"),
    )
    return jax.shard_map(
        shards,
        mesh=mesh,
        in_specs=placed,
        out_specs=(P("dp", "mp"), P("dp", "mp"), P("dp", "mp"), P(("dp", "mp"), None)),
        check_vma=False,
    )
```

profile of v0, /device:TPU:2, one launch (start us, length us, event | category | flops | bytes accessed | tf_op | source)
XLA Modules:
  0.0 178.7 jit_solution(14542377256666155833)
XLA Ops:
  13.3 1.7 collective-permute-start.1
  15.0 11.6 %all-to-all-start = ((bf16[32,2,16,128]{3,2,1,0:T(8,128)(2,1)}), bf16[32,2,16,128]{3,2,1,0:T(8,128)(2,1)S(1)}, u32[]{:S(2)}, u32[]{:S(2)}) async-start(bf16[32,2,16,128]{3,2,1,0:T(8,128)(2,1)} %get-tuple-element.48), calls=%async_computation | async-start | bytes 524288 | tf_op jit(solution)/shard_map/slot_grads_spread/all_to_all | solution.py:598
  26.6 1.7 collective-permute-start.3
  28.3 9.4 %collective-permute-done.3.refs_3_.refs_5_ = bf16[32,3200]{1,0:T(8,128)(2,1)S(1)} collective-permute-done((bf16[32,3200]{1,0:T(8,128)(2,1)S(1)}, bf16[32,3200]{1,0:T(8,128)(2,1)S(1)}, u32[]{:S(2)}, u32[]{:S(2)}) %collective-permute-start.3) | collective-permute-done | bytes 204832 | tf_op jit(solution)/shard_map/vision_gather/ppermute | solution.py:548
  39.1 9.9 %all-to-all-start.1 = ((bf16[32,16,128]{2,1,0:T(8,128)(2,1)}), bf16[32,16,128]{2,1,0:T(8,128)(2,1)S(1)}, u32[]{:S(2)}, u32[]{:S(2)}) async-start(bf16[32,16,128]{2,1,0:T(8,128)(2,1)} %get-tuple-element.58), calls=%async_computation.2 | async-start | bytes 262144 | tf_op jit(solution)/shard_map/slot_grads_collect/all_to_all | solution.py:605
  49.1 9.8 %image_forward.1 = (bf16[256,1024]{1,0:T(8,128)(2,1)}, bf16[4,256,256]{2,1,0:T(8,128)(2,1)}, f32[4,256,256]{2,1,0:T(8,128)}, f32[2,128]{1,0:T(2,128)S(1)}, f32[8,128]{1,0:T(8,128)S(1)}) custom-call(s32[8]{0:T(128)S(1)} %stack.35.refs_0_, s32[8]{0:T(128)S(1)} %fusion.2.refs_1_.refs_0_, bf16[64,3200]{1,0:T(8,128)(2,1)S(1)} %join.2.refs_2_, ...), custom_call_target="tpu_custom_call" | custom-call | flops 2751463424 | bytes 14488640 | tf_op jit(solution)/shard_map/image_forward/pallas_call | solution.py:61
  61.3 7.7 %text_forward.1 = (bf16[8,512,256]{2,1,0:T(8,128)(2,1)}, f32[4,128]{1,0:T(4,128)S(1)}, f32[8,128]{1,0:T(8,128)S(1)}) custom-call(bf16[512,1024]{1,0:T(8,128)(2,1)S(1)} %copy-done.3, f32[1,1024]{1,0:T(1,128)S(1)} %bitcast.29, bf16[1024,1024]{1,0:T(8,128)(2,1)} %refs_6_.1, bf16[1024,1024]{1,0:T(8,128)(2,1)} %refs_7_.3, f32[8,128]{1,0:T(8,128)S(1)} %get-tuple-element.51.refs_4_), custom_call_target="tpu_custom_call" | custom-call | flops 2147483648 | bytes 7346176 | tf_op jit(solution)/shard_map/text_forward/pallas_call | solution.py:61
  72.9 1.9 %collective-permute-start.10 = (bf16[256,256]{1,0:T(8,128)(2,1)S(1)}, bf16[256,256]{1,0:T(8,128)(2,1)S(1)}, u32[]{:S(2)}, u32[]{:S(2)}) collective-permute-start(bf16[256,256]{1,0:T(8,128)(2,1)S(1)} %get-tuple-element.61), channel_id=1, source_target_pairs={{0,6},{1,7},{2,0},{3,1},{4,2},{5,3},{6,4},{7,5},{8,14},{9,15},{10,... | collective-permute-start | bytes 393224 | tf_op jit(solution)/shard_map/image_key_value_sum/ppermute | solution.py:34
  76.5 1.8 collective-permute-done.10.refs_2_.refs_8_
  78.3 3.2 %collective-permute-start.12 = (bf16[128,256]{1,0:T(8,128)(2,1)S(1)}, bf16[128,256]{1,0:T(8,128)(2,1)S(1)}, u32[]{:S(2)}, u32[]{:S(2)}) collective-permute-start(bf16[128,256]{1,0:T(8,128)(2,1)S(1)} %add_convert_fusion.2), channel_id=1, source_target_pairs={{0,6},{1,7},{2,0},{3,1},{4,2},{5,3},{6,4},{7,5},{8,14},{9,15},{10,... | collective-permute-start | bytes 196616 | tf_op jit(solution)/shard_map/image_key_value_sum/ppermute | solution.py:34
  81.6 4.8 %collective-permute-done.6 = f32[6,128]{1,0:T(8,128)S(1)} collective-permute-done((f32[6,128]{1,0:T(8,128)S(1)}, f32[6,128]{1,0:T(8,128)S(1)}, u32[]{:S(2)}, u32[]{:S(2)}) %collective-permute-start.6) | collective-permute-done | bytes 3104 | tf_op jit(solution)/shard_map/squares_sum/ppermute | solution.py:30
  86.5 5.1 %collective-permute-done.7 = f32[6,128]{1,0:T(8,128)S(1)} collective-permute-done((f32[6,128]{1,0:T(8,128)S(1)}, f32[6,128]{1,0:T(8,128)S(1)}, u32[]{:S(2)}, u32[]{:S(2)}) %collective-permute-start.7) | collective-permute-done | bytes 3104 | tf_op jit(solution)/shard_map/squares_sum/ppermute | solution.py:38
  92.5 9.8 %all-to-all-start.2 = ((bf16[32,16,128]{2,1,0:T(8,128)(2,1)}), bf16[32,16,128]{2,1,0:T(8,128)(2,1)S(1)}, u32[]{:S(2)}, u32[]{:S(2)}) async-start(bf16[32,16,128]{2,1,0:T(8,128)(2,1)} %bitcast.14), calls=%async_computation.3 | async-start | bytes 262144 | tf_op jit(solution)/shard_map/image_out_spread/all_to_all | solution.py:623
  102.4 8.7 %backward.2 = (f32[512,1024]{1,0:T(8,128)}, f32[4,128]{1,0:T(4,128)S(1)}, f32[8,128]{1,0:T(8,128)S(1)}) custom-call(s32[8]{0:T(128)S(1)} %iota.20.refs_0_, bf16[8192,128]{1,0:T(8,128)(2,1)} %all-gather.2.cloned.1.call-done.refs_1_, bf16[1024,1024]{1,0:T(8,128)(2,1)} %refs_6_.1, bf16[1024,1024]{1,0:T(8,128)(2,1)} %refs_7_.3, f32[1,1024]{1,0:T(1,128)S(1)} %bitcast.30, ...), custom_call_target="tpu_custom_call" | custom-call | flops 2147483648 | bytes 9443360 | tf_op jit(solution)/shard_map/backward/pallas_call | solution.py:61
  111.1 6.4 %backward.3 = (f32[256,1024]{1,0:T(8,128)}, f32[2,128]{1,0:T(2,128)S(1)}, f32[8,128]{1,0:T(8,128)}) custom-call(s32[8]{0:T(128)S(1)} %stack.35.refs_0_, bf16[1024,128]{1,0:T(8,128)(2,1)S(1)} %join.3.refs_1_, bf16[1024,128]{1,0:T(8,128)(2,1)S(1)} %collective-permute-done.14.refs_2_, bf16[1024,128]{1,0:T(8,128)(2,1)S(1)} %collective-permute-done.15.refs_3_, ...), custom_call_target="tpu_custom_call" | custom-call | flops 1073741824 | bytes 6820896 | tf_op jit(solution)/shard_map/backward/pallas_call | solution.py:61
  118.9 4.8 %collective-permute-done.19 = f32[6,128]{1,0:T(8,128)S(1)} collective-permute-done((f32[6,128]{1,0:T(8,128)S(1)}, f32[6,128]{1,0:T(8,128)S(1)}, u32[]{:S(2)}, u32[]{:S(2)}) %collective-permute-start.19) | collective-permute-done | bytes 3104 | tf_op jit(solution)/shard_map/inner_sum/ppermute | solution.py:30
  123.7 5.1 %collective-permute-done.20 = f32[6,128]{1,0:T(8,128)S(1)} collective-permute-done((f32[6,128]{1,0:T(8,128)S(1)}, f32[6,128]{1,0:T(8,128)S(1)}, u32[]{:S(2)}, u32[]{:S(2)}) %collective-permute-start.20) | collective-permute-done | bytes 3104 | tf_op jit(solution)/shard_map/inner_sum/ppermute | solution.py:38
  128.8 7.6 %image_backward.1 = (bf16[128,3200]{1,0:T(8,128)(2,1)}, f32[128,3200]{1,0:T(8,128)}, f32[8,128]{1,0:T(8,128)S(1)}) custom-call(s32[8]{0:T(128)S(1)} %fusion.2.refs_1_.refs_0_, f32[256,1024]{1,0:T(8,128)} %get-tuple-element.70.refs_1_, bf16[256,1024]{1,0:T(8,128)(2,1)S(1)} %copy-done, f32[2,128]{1,0:T(2,128)S(1)} %slice.31.refs_5_.refs_3_, ...), custom_call_target="tpu_custom_call" | custom-call | flops 1677721600 | bytes 10586144 | tf_op jit(solution)/shard_map/image_backward/pallas_call | solution.py:61
  136.7 2.4 %collective-permute-done.21 = bf16[128,3200]{1,0:T(8,128)(2,1)S(1)} collective-permute-done((bf16[128,3200]{1,0:T(8,128)(2,1)}, bf16[128,3200]{1,0:T(8,128)(2,1)S(1)}, u32[]{:S(2)}, u32[]{:S(2)}) %collective-permute-start.21) | collective-permute-done | bytes 819232 | tf_op jit(solution)/shard_map/d_vis_sum/ppermute | solution.py:42
  143.3 9.8 %all-to-all-start.3 = ((bf16[32,2,16,128]{3,2,1,0:T(8,128)(2,1)}), bf16[32,2,16,128]{3,2,1,0:T(8,128)(2,1)S(1)}, u32[]{:S(2)}, u32[]{:S(2)}) async-start(bf16[32,2,16,128]{3,2,1,0:T(8,128)(2,1)} %bitcast.19), calls=%async_computation.4 | async-start | bytes 524288 | tf_op jit(solution)/shard_map/image_out_collect/all_to_all | solution.py:640
  153.1 3.3 %collective-permute-start.23 = (bf16[32,3200]{1,0:T(8,128)(2,1)}, bf16[32,3200]{1,0:T(8,128)(2,1)S(1)}, u32[]{:S(2)}, u32[]{:S(2)}) collective-permute-start(bf16[32,3200]{1,0:T(8,128)(2,1)} %copy-done.11), channel_id=1, source_target_pairs={{0,6},{1,7},{2,0},{3,1},{4,2},{5,3},{6,4},{7,5},{8,14},{9,15},{10,... | collective-permute-start | bytes 614408 | tf_op jit(solution)/shard_map/d_vis_sum/ppermute | solution.py:34
  156.6 4.0 %collective-permute-done.23.refs_7_.refs_2_ = bf16[32,3200]{1,0:T(8,128)(2,1)S(1)} collective-permute-done((bf16[32,3200]{1,0:T(8,128)(2,1)}, bf16[32,3200]{1,0:T(8,128)(2,1)S(1)}, u32[]{:S(2)}, u32[]{:S(2)}) %collective-permute-start.23) | collective-permute-done | bytes 204832 | tf_op jit(solution)/shard_map/d_vis_sum/ppermute | solution.py:34
  160.6 3.7 %collective-permute-start.25 = (bf16[16,3200]{1,0:T(8,128)(2,1)S(1)}, bf16[16,3200]{1,0:T(8,128)(2,1)S(1)}, u32[]{:S(2)}, u32[]{:S(2)}) collective-permute-start(bf16[16,3200]{1,0:T(8,128)(2,1)S(1)} %add_convert_fusion), channel_id=1, source_target_pairs={{0,6},{1,7},{2,0},{3,1},{4,2},{5,3},{6,4},{7,5},{8,14},{9,15},{10,... | collective-permute-start | bytes 307208 | tf_op jit(solution)/shard_map/d_vis_sum/ppermute | solution.py:34
  164.5 3.9 %text_out.1 = (bf16[512,1024]{1,0:T(8,128)(2,1)}, f32[8,128]{1,0:T(8,128)}) custom-call(s32[2]{0:T(128)S(1)} %convert_element_type.27.refs_0_, f32[512,1024]{1,0:T(8,128)} %get-tuple-element.79.refs_1_, bf16[512,1024]{1,0:T(8,128)(2,1)S(1)} %copy-done.3, f32[4,128]{1,0:T(4,128)S(1)} %slice.28.refs_2_.refs_3_, f32[4,128]{1,0:T(4,128)S(1)} %slice.33.refs_4_, ...), custom_call_target="tpu_custom_call" | custom-call | bytes 4198408 | tf_op jit(solution)/shard_map/text_out/pallas_call | solution.py:61
  (110 shorter events, 26.1 us)
Async XLA Ops:
  7.2 95.2 %all-gather.2.cloned.1.call-start = ((), (), s32[]{:S(2)}) async-start(), calls=%async_computation.6 | async-start | bytes 2359296 | tf_op jit(solution)/shard_map/text_grad_gather/all_gather | solution.py:600
  13.3 13.3 %collective-permute-start.1 = (bf16[64,3200]{1,0:T(8,128)(2,1)S(1)}, bf16[64,3200]{1,0:T(8,128)(2,1)S(1)}, u32[]{:S(2)}, u32[]{:S(2)}) collective-permute-start(bf16[64,3200]{1,0:T(8,128)(2,1)S(1)} %join.2.refs_2_), channel_id=1, source_target_pairs={{0,2},{1,7},{2,4},{3,1},{4,6},{5,3},{6,0},{7,5},{8,10},{9,15},{10,... | collective-permute-start | bytes 1228808 | tf_op jit(solution)/shard_map/vision_gather/ppermute | solution.py:547
  15.0 22.9 %all-to-all-start = ((bf16[32,2,16,128]{3,2,1,0:T(8,128)(2,1)}), bf16[32,2,16,128]{3,2,1,0:T(8,128)(2,1)S(1)}, u32[]{:S(2)}, u32[]{:S(2)}) async-start(bf16[32,2,16,128]{3,2,1,0:T(8,128)(2,1)} %get-tuple-element.48), calls=%async_computation | async-start | bytes 524288 | tf_op jit(solution)/shard_map/slot_grads_spread/all_to_all | solution.py:598
  26.6 11.0 %collective-permute-start.3 = (bf16[32,3200]{1,0:T(8,128)(2,1)S(1)}, bf16[32,3200]{1,0:T(8,128)(2,1)S(1)}, u32[]{:S(2)}, u32[]{:S(2)}) collective-permute-start(bf16[32,3200]{1,0:T(8,128)(2,1)S(1)} %constant_dynamic-slice_fusion.1), channel_id=1, source_target_pairs={{0,2},{1,7},{2,4},{3,1},{4,6},{5,3},{6,0},{7,5},{8,10},{9,15},{10,... | collective-permute-start | bytes 614408 | tf_op jit(solution)/shard_map/vision_gather/ppermute | solution.py:548
  28.3 20.8 %collective-permute-start.2 = (bf16[64,3200]{1,0:T(8,128)(2,1)S(1)}, bf16[64,3200]{1,0:T(8,128)(2,1)S(1)}, u32[]{:S(2)}, u32[]{:S(2)}) collective-permute-start(bf16[64,3200]{1,0:T(8,128)(2,1)S(1)} %collective-permute-done.1.refs_3_), channel_id=1, source_target_pairs={{0,1},{1,0},{2,3},{3,2},{4,5},{5,4},{6,7},{7,6},{8,9},{9,8},{10,11... | collective-permute-start | bytes 1228808 | tf_op jit(solution)/shard_map/vision_gather/ppermute | solution.py:42
  37.7 11.4 %collective-permute-start.4 = (bf16[32,3200]{1,0:T(8,128)(2,1)S(1)}, bf16[32,3200]{1,0:T(8,128)(2,1)S(1)}, u32[]{:S(2)}, u32[]{:S(2)}) collective-permute-start(bf16[32,3200]{1,0:T(8,128)(2,1)S(1)} %collective-permute-done.3.refs_3_.refs_5_), channel_id=1, source_target_pairs={{0,1},{1,0},{2,3},{3,2},{4,5},{5,4},{6,7},{7,6},{8,9},{9,8},{10,11... | collective-permute-start | bytes 614408 | tf_op jit(solution)/shard_map/vision_gather/ppermute | solution.py:42
  39.1 19.9 %all-to-all-start.1 = ((bf16[32,16,128]{2,1,0:T(8,128)(2,1)}), bf16[32,16,128]{2,1,0:T(8,128)(2,1)S(1)}, u32[]{:S(2)}, u32[]{:S(2)}) async-start(bf16[32,16,128]{2,1,0:T(8,128)(2,1)} %get-tuple-element.58), calls=%async_computation.2 | async-start | bytes 262144 | tf_op jit(solution)/shard_map/slot_grads_collect/all_to_all | solution.py:605
  49.0 120.4 %reduce-scatter.2.cloned.1.call-start = ((), (), s32[]{:S(2)}) async-start(), calls=%async_computation.5 | async-start | bytes 2359296 | tf_op jit(solution)/shard_map/text_key_value_sum/reduce_scatter | solution.py:612
  58.9 10.1 %collective-permute-start.8 = (bf16[4,256,256]{2,1,0:T(8,128)(2,1)}, bf16[4,256,256]{2,1,0:T(8,128)(2,1)S(1)}, u32[]{:S(2)}, u32[]{:S(2)}) collective-permute-start(bf16[4,256,256]{2,1,0:T(8,128)(2,1)} %get-tuple-element.56), channel_id=1, source_target_pairs={{0,1},{1,0},{2,3},{3,2},{4,5},{5,4},{6,7},{7,6},{8,9},{9,8},{10,11... | collective-permute-start | bytes 1572872 | tf_op jit(solution)/shard_map/image_key_value_sum/ppermute | solution.py:42
  61.1 9.7 %collective-permute-start.14 = (bf16[1024,128]{1,0:T(8,128)(2,1)S(1)}, bf16[1024,128]{1,0:T(8,128)(2,1)S(1)}, u32[]{:S(2)}, u32[]{:S(2)}) collective-permute-start(bf16[1024,128]{1,0:T(8,128)(2,1)S(1)} %join.3.refs_1_), channel_id=1, source_target_pairs={{0,2},{1,7},{2,4},{3,1},{4,6},{5,3},{6,0},{7,5},{8,10},{9,15},{10,... | collective-permute-start | bytes 786440 | tf_op jit(solution)/shard_map/image_grad_gather/ppermute | solution.py:547
  69.1 7.1 %collective-permute-start.9 = (bf16[256,256]{1,0:T(8,128)(2,1)S(1)}, bf16[256,256]{1,0:T(8,128)(2,1)S(1)}, u32[]{:S(2)}, u32[]{:S(2)}) collective-permute-start(bf16[256,256]{1,0:T(8,128)(2,1)S(1)} %get-tuple-element.60), channel_id=1, source_target_pairs={{0,2},{1,3},{2,4},{3,5},{4,6},{5,7},{6,0},{7,1},{8,10},{9,11},{10,... | collective-permute-start | bytes 393224 | tf_op jit(solution)/shard_map/image_key_value_sum/ppermute | solution.py:30
  70.8 10.8 %collective-permute-start.5 = (f32[6,128]{1,0:T(8,128)S(1)}, f32[6,128]{1,0:T(8,128)S(1)}, u32[]{:S(2)}, u32[]{:S(2)}) collective-permute-start(f32[6,128]{1,0:T(8,128)S(1)} %pad_maximum_fusion), channel_id=1, source_target_pairs={{0,1},{1,0},{2,3},{3,2},{4,5},{5,4},{6,7},{7,6},{8,9},{9,8},{10,11... | collective-permute-start | bytes 9224 | tf_op jit(solution)/shard_map/squares_sum/ppermute | solution.py:42
  70.8 20.7 %collective-permute-start.16 = (bf16[512,128]{1,0:T(8,128)(2,1)S(1)}, bf16[512,128]{1,0:T(8,128)(2,1)S(1)}, u32[]{:S(2)}, u32[]{:S(2)}) collective-permute-start(bf16[512,128]{1,0:T(8,128)(2,1)S(1)} %constant_dynamic-slice_fusion), channel_id=1, source_target_pairs={{0,2},{1,7},{2,4},{3,1},{4,6},{5,3},{6,0},{7,5},{8,10},{9,15},{10,... | collective-permute-start | bytes 393224 | tf_op jit(solution)/shard_map/image_grad_gather/ppermute | solution.py:548
  71.3 39.8 %collective-permute-start.15 = (bf16[1024,128]{1,0:T(8,128)(2,1)S(1)}, bf16[1024,128]{1,0:T(8,128)(2,1)S(1)}, u32[]{:S(2)}, u32[]{:S(2)}) collective-permute-start(bf16[1024,128]{1,0:T(8,128)(2,1)S(1)} %collective-permute-done.14.refs_2_), channel_id=1, source_target_pairs={{0,1},{1,0},{2,3},{3,2},{4,5},{5,4},{6,7},{7,6},{8,9},{9,8},{10,11... | collective-permute-start | bytes 786440 | tf_op jit(solution)/shard_map/image_grad_gather/ppermute | solution.py:42
  72.9 5.4 %collective-permute-start.10 = (bf16[256,256]{1,0:T(8,128)(2,1)S(1)}, bf16[256,256]{1,0:T(8,128)(2,1)S(1)}, u32[]{:S(2)}, u32[]{:S(2)}) collective-permute-start(bf16[256,256]{1,0:T(8,128)(2,1)S(1)} %get-tuple-element.61), channel_id=1, source_target_pairs={{0,6},{1,7},{2,0},{3,1},{4,2},{5,3},{6,4},{7,5},{8,14},{9,15},{10,... | collective-permute-start | bytes 393224 | tf_op jit(solution)/shard_map/image_key_value_sum/ppermute | solution.py:34
  76.2 15.5 %collective-permute-start.11 = (bf16[128,256]{1,0:T(8,128)(2,1)S(1)}, bf16[128,256]{1,0:T(8,128)(2,1)S(1)}, u32[]{:S(2)}, u32[]{:S(2)}) collective-permute-start(bf16[128,256]{1,0:T(8,128)(2,1)S(1)} %add_convert_fusion.3), channel_id=1, source_target_pairs={{0,2},{1,3},{2,4},{3,5},{4,6},{5,7},{6,0},{7,1},{8,10},{9,11},{10,... | collective-permute-start | bytes 196616 | tf_op jit(solution)/shard_map/image_key_value_sum/ppermute | solution.py:30
  78.3 13.4 %collective-permute-start.12 = (bf16[128,256]{1,0:T(8,128)(2,1)S(1)}, bf16[128,256]{1,0:T(8,128)(2,1)S(1)}, u32[]{:S(2)}, u32[]{:S(2)}) collective-permute-start(bf16[128,256]{1,0:T(8,128)(2,1)S(1)} %add_convert_fusion.2), channel_id=1, source_target_pairs={{0,6},{1,7},{2,0},{3,1},{4,2},{5,3},{6,4},{7,5},{8,14},{9,15},{10,... | collective-permute-start | bytes 196616 | tf_op jit(solution)/shard_map/image_key_value_sum/ppermute | solution.py:34
  91.6 19.5 %collective-permute-start.17 = (bf16[512,128]{1,0:T(8,128)(2,1)S(1)}, bf16[512,128]{1,0:T(8,128)(2,1)S(1)}, u32[]{:S(2)}, u32[]{:S(2)}) collective-permute-start(bf16[512,128]{1,0:T(8,128)(2,1)S(1)} %collective-permute-done.16.refs_4_), channel_id=1, source_target_pairs={{0,1},{1,0},{2,3},{3,2},{4,5},{5,4},{6,7},{7,6},{8,9},{9,8},{10,11... | collective-permute-start | bytes 393224 | tf_op jit(solution)/shard_map/image_grad_gather/ppermute | solution.py:42
  92.5 36.3 %all-to-all-start.2 = ((bf16[32,16,128]{2,1,0:T(8,128)(2,1)}), bf16[32,16,128]{2,1,0:T(8,128)(2,1)S(1)}, u32[]{:S(2)}, u32[]{:S(2)}) async-start(bf16[32,16,128]{2,1,0:T(8,128)(2,1)} %bitcast.14), calls=%async_computation.3 | async-start | bytes 262144 | tf_op jit(solution)/shard_map/image_out_spread/all_to_all | solution.py:623
  142.0 14.5 %collective-permute-start.22 = (bf16[32,3200]{1,0:T(8,128)(2,1)}, bf16[32,3200]{1,0:T(8,128)(2,1)S(1)}, u32[]{:S(2)}, u32[]{:S(2)}) collective-permute-start(bf16[32,3200]{1,0:T(8,128)(2,1)} %get-tuple-element.81), channel_id=1, source_target_pairs={{0,2},{1,3},{2,4},{3,5},{4,6},{5,7},{6,0},{7,1},{8,10},{9,11},{10,... | collective-permute-start | bytes 614408 | tf_op jit(solution)/shard_map/d_vis_sum/ppermute | solution.py:30
  143.3 26.1 %all-to-all-start.3 = ((bf16[32,2,16,128]{3,2,1,0:T(8,128)(2,1)}), bf16[32,2,16,128]{3,2,1,0:T(8,128)(2,1)S(1)}, u32[]{:S(2)}, u32[]{:S(2)}) async-start(bf16[32,2,16,128]{3,2,1,0:T(8,128)(2,1)} %bitcast.19), calls=%async_computation.4 | async-start | bytes 524288 | tf_op jit(solution)/shard_map/image_out_collect/all_to_all | solution.py:640
  153.1 7.4 %collective-permute-start.23 = (bf16[32,3200]{1,0:T(8,128)(2,1)}, bf16[32,3200]{1,0:T(8,128)(2,1)S(1)}, u32[]{:S(2)}, u32[]{:S(2)}) collective-permute-start(bf16[32,3200]{1,0:T(8,128)(2,1)} %copy-done.11), channel_id=1, source_target_pairs={{0,6},{1,7},{2,0},{3,1},{4,2},{5,3},{6,4},{7,5},{8,14},{9,15},{10,... | collective-permute-start | bytes 614408 | tf_op jit(solution)/shard_map/d_vis_sum/ppermute | solution.py:34
  156.5 11.9 %collective-permute-start.24 = (bf16[16,3200]{1,0:T(8,128)(2,1)S(1)}, bf16[16,3200]{1,0:T(8,128)(2,1)S(1)}, u32[]{:S(2)}, u32[]{:S(2)}) collective-permute-start(bf16[16,3200]{1,0:T(8,128)(2,1)S(1)} %add_convert_fusion.1), channel_id=1, source_target_pairs={{0,2},{1,3},{2,4},{3,5},{4,6},{5,7},{6,0},{7,1},{8,10},{9,11},{10,... | collective-permute-start | bytes 307208 | tf_op jit(solution)/shard_map/d_vis_sum/ppermute | solution.py:30
  160.6 7.8 %collective-permute-start.25 = (bf16[16,3200]{1,0:T(8,128)(2,1)S(1)}, bf16[16,3200]{1,0:T(8,128)(2,1)S(1)}, u32[]{:S(2)}, u32[]{:S(2)}) collective-permute-start(bf16[16,3200]{1,0:T(8,128)(2,1)S(1)} %add_convert_fusion), channel_id=1, source_target_pairs={{0,6},{1,7},{2,0},{3,1},{4,2},{5,3},{6,4},{7,5},{8,14},{9,15},{10,... | collective-permute-start | bytes 307208 | tf_op jit(solution)/shard_map/d_vis_sum/ppermute | solution.py:34
  (20 other events, 146.6 us)
Sparse Core Ops, SparseCore 0:
  11.9 31.7 all-gather.1
  70.9 37.5 reduce-scatter.1
where the time goes:
time: 179 us
  starting transfers between devices  61.9 us (35%)
  Pallas kernels  51.9 us (29%)
  waiting for transfers between devices  43.1 us (24%)
  between operations  14.6 us (8%)
  local copies, waits for them, and re-layouts  6.7 us (4%)
    pallas_call x17, Pallas kernels, call(): pl.pallas_call(body, in_specs=[SMEM if i < scalars else HBM if i in far e...  51.9 us
    ppermute x4, starting transfers between devices, down(): return lax.ppermute(x, 'mp', DOWN)  12.1 us
    all_to_all x1, starting transfers between devices, shards(): lax.all_to_all(grad_chunks, 'dp', split_axis=0, concat_axis=0, tiled=True)  11.6 us
    ppermute x6, waiting for transfers between devices, up(): return lax.ppermute(x, 'mp', UP)  11 us
    ppermute x2, waiting for transfers between devices, across(): return lax.ppermute(x, 'mp', ACROSS)  10.2 us
    all_to_all x1, starting transfers between devices, shards(): lax.all_to_all(picked, 'dp', split_axis=0, concat_axis=0, tiled=True)  9.87 us
    all_to_all x1, starting transfers between devices, shards(): lax.all_to_all(packed.reshape(dp, slots, CHUNK, LANE), 'dp', split_axis=0...  9.81 us
    all_to_all x1, starting transfers between devices, shards(): lax.all_to_all(image_kv.reshape(dp, CHUNK, LANE), 'dp', split_axis=0, con...  9.79 us
  transfers between devices with their start and end apart: 32, of which 13 were waited for; matrix products, arithmetic and copies ran while one was open for 0% of the time, Pallas kernels for 28%

commit v1 on v0

--- a/solution.py
+++ b/solution.py
@@ -551,8 +551,7 @@
 
 def small_sum(x):
     pair = x + peer(x)
-    pair = pair + up(pair)
-    return pair + across(pair)
+    return (pair + up(pair)) + (down(pair) + across(pair))
 
 
 def shards(
@@ -627,11 +626,11 @@
     text_d, text_inner, text_back = backward(
         rel, [text_g], w_key, w_value, gain, text_embed, [kv_ring, pieces[1], pieces[2]]
     )
-    image_d, image_inner, _ = backward(where, image_g, w_key, w_value, gain, embed, [text_back, kv_out])
+    image_d, image_inner, _ = backward(where, image_g, w_key, w_value, gain, embed, [text_back, spread])
     with jax.named_scope("inner_sum"):
         inner = small_sum(jnp.concatenate([text_inner, image_inner]))
     d_far, d_near, back_done = image_backward(
-        order, image_d, embed, image_square, inner[text_rows:], w_proj, [spread]
+        order, image_d, embed, image_square, inner[text_rows:], w_proj, [kv_out]
     )
     with jax.named_scope("d_vis_sum"):
         d_pieces, d_ring = ring_sum(d_near.reshape(RING, -1, DV), d_far)

time: 179 us -> 177 us (0.989)
  waiting for transfers between devices: 43.1 us -> 31.3 us
  starting transfers between devices: 61.9 us -> 69.7 us
    ppermute x6, waiting for transfers between devices: 11 us -> 4.03 us  [up(): return lax.ppermute(x, 'mp', UP)]
    ppermute x2, waiting for transfers between devices: 10.2 us -> 3.58 us  [across(): return lax.ppermute(x, 'mp', ACROSS)]
    ppermute x4 -> x6, starting transfers between devices: 12.1 us -> 18.6 us  [down(): return lax.ppermute(x, 'mp', DOWN)]
    ppermute x4 -> x6, waiting for transfers between devices: 5.75 us -> 7.68 us  [down(): return lax.ppermute(x, 'mp', DOWN)]
    ppermute x10, waiting for transfers between devices: 6.61 us -> 4.78 us  [peer(): return lax.ppermute(x, 'mp', PEER)]
  transfers between devices with their start and end apart: 32 -> 34, of which waited for: 13 -> 12; matrix products, arithmetic and copies ran while one was open for 0% -> 0% of each run, Pallas kernels for 28% -> 29%
where the time goes in v1:
time: 177 us; the launch traced here: 176 us
  starting transfers between devices  69.7 us (39%)
  Pallas kernels  52.9 us (30%)
  waiting for transfers between devices  31.3 us (18%)
  between operations  14.5 us (8%)
  local copies, waits for them, and re-layouts  7.34 us (4%)
    pallas_call x17, Pallas kernels, call(): pl.pallas_call(body, in_specs=[SMEM if i < scalars else HBM if i in far e...  52.9 us
    ppermute x6, starting transfers between devices, down(): return lax.ppermute(x, 'mp', DOWN)  18.6 us
    all_to_all x1, starting transfers between devices, shards(): lax.all_to_all(grad_chunks, 'dp', split_axis=0, concat_axis=0, tiled=True)  11.6 us
    all_to_all x1, starting transfers between devices, shards(): lax.all_to_all(image_kv.reshape(dp, CHUNK, LANE), 'dp', split_axis=0, con...  10.1 us
    all_to_all x1, starting transfers between devices, shards(): lax.all_to_all(picked, 'dp', split_axis=0, concat_axis=0, tiled=True)  9.87 us
    all_to_all x1, starting transfers between devices, shards(): lax.all_to_all(packed.reshape(dp, slots, CHUNK, LANE), 'dp', split_axis=0...  9.66 us
    ppermute x2, waiting for transfers between devices, chip_gather(): lax.ppermute(lax.dynamic_slice_in_dim(near, core[0] * rows, rows), 'mp',...  9.37 us
    ppermute x6, waiting for transfers between devices, down(): return lax.ppermute(x, 'mp', DOWN)  7.68 us
  transfers between devices with their start and end apart: 34, of which 12 were waited for; matrix products, arithmetic and copies ran while one was open for 0% of the time, Pallas kernels for 29%

profile of v1, /device:TPU:2, one launch (start us, length us, event | category | flops | bytes accessed | tf_op | source)
XLA Modules:
  0.0 176.2 jit_solution(3554113266817395366)
XLA Ops:
  13.3 1.7 collective-permute-start.1
  15.0 11.6 %all-to-all-start = ((bf16[32,2,16,128]{3,2,1,0:T(8,128)(2,1)}), bf16[32,2,16,128]{3,2,1,0:T(8,128)(2,1)S(1)}, u32[]{:S(2)}, u32[]{:S(2)}) async-start(bf16[32,2,16,128]{3,2,1,0:T(8,128)(2,1)} %get-tuple-element.48), calls=%async_computation | async-start | bytes 524288 | tf_op jit(solution)/shard_map/slot_grads_spread/all_to_all | solution.py:597
  26.6 1.7 collective-permute-start.3
  28.3 9.4 %collective-permute-done.3.refs_3_.refs_5_ = bf16[32,3200]{1,0:T(8,128)(2,1)S(1)} collective-permute-done((bf16[32,3200]{1,0:T(8,128)(2,1)S(1)}, bf16[32,3200]{1,0:T(8,128)(2,1)S(1)}, u32[]{:S(2)}, u32[]{:S(2)}) %collective-permute-start.3) | collective-permute-done | bytes 204832 | tf_op jit(solution)/shard_map/vision_gather/ppermute | solution.py:548
  39.1 9.9 %all-to-all-start.1 = ((bf16[32,16,128]{2,1,0:T(8,128)(2,1)}), bf16[32,16,128]{2,1,0:T(8,128)(2,1)S(1)}, u32[]{:S(2)}, u32[]{:S(2)}) async-start(bf16[32,16,128]{2,1,0:T(8,128)(2,1)} %get-tuple-element.58), calls=%async_computation.2 | async-start | bytes 262144 | tf_op jit(solution)/shard_map/slot_grads_collect/all_to_all | solution.py:604
  49.1 9.8 %image_forward.1 = (bf16[256,1024]{1,0:T(8,128)(2,1)}, bf16[4,256,256]{2,1,0:T(8,128)(2,1)}, f32[4,256,256]{2,1,0:T(8,128)}, f32[2,128]{1,0:T(2,128)S(1)}, f32[8,128]{1,0:T(8,128)S(1)}) custom-call(s32[8]{0:T(128)S(1)} %stack.35.refs_0_, s32[8]{0:T(128)S(1)} %fusion.2.refs_1_.refs_0_, bf16[64,3200]{1,0:T(8,128)(2,1)S(1)} %join.2.refs_2_, ...), custom_call_target="tpu_custom_call" | custom-call | flops 2751463424 | bytes 14488640 | tf_op jit(solution)/shard_map/image_forward/pallas_call | solution.py:61
  59.5 7.7 %text_forward.1 = (bf16[8,512,256]{2,1,0:T(8,128)(2,1)}, f32[4,128]{1,0:T(4,128)S(1)}, f32[8,128]{1,0:T(8,128)S(1)}) custom-call(bf16[512,1024]{1,0:T(8,128)(2,1)S(1)} %copy-done.3, f32[1,1024]{1,0:T(1,128)S(1)} %bitcast.29, bf16[1024,1024]{1,0:T(8,128)(2,1)} %refs_6_.1, bf16[1024,1024]{1,0:T(8,128)(2,1)} %refs_7_.3, f32[8,128]{1,0:T(8,128)S(1)} %get-tuple-element.51.refs_4_), custom_call_target="tpu_custom_call" | custom-call | flops 2147483648 | bytes 7346176 | tf_op jit(solution)/shard_map/text_forward/pallas_call | solution.py:61
  70.4 2.5 %collective-permute-start.7 = (f32[6,128]{1,0:T(8,128)S(1)}, f32[6,128]{1,0:T(8,128)S(1)}, u32[]{:S(2)}, u32[]{:S(2)}) collective-permute-start(f32[6,128]{1,0:T(8,128)S(1)} %fusion.6), channel_id=1, source_target_pairs={{0,6},{1,7},{2,0},{3,1},{4,2},{5,3},{6,4},{7,5},{8,14},{9,15},{10,... | collective-permute-start | bytes 9224 | tf_op jit(solution)/shard_map/squares_sum/ppermute | solution.py:34
  77.8 1.7 collective-permute-start.11
  79.6 3.7 %collective-permute-done.11.refs_2_.refs_8_ = bf16[256,256]{1,0:T(8,128)(2,1)S(1)} collective-permute-done((bf16[256,256]{1,0:T(8,128)(2,1)S(1)}, bf16[256,256]{1,0:T(8,128)(2,1)S(1)}, u32[]{:S(2)}, u32[]{:S(2)}) %collective-permute-start.11) | collective-permute-done | bytes 131104 | tf_op jit(solution)/shard_map/image_key_value_sum/ppermute | solution.py:34
  83.4 3.7 %collective-permute-start.13 = (bf16[128,256]{1,0:T(8,128)(2,1)S(1)}, bf16[128,256]{1,0:T(8,128)(2,1)S(1)}, u32[]{:S(2)}, u32[]{:S(2)}) collective-permute-start(bf16[128,256]{1,0:T(8,128)(2,1)S(1)} %add_convert_fusion.2), channel_id=1, source_target_pairs={{0,6},{1,7},{2,0},{3,1},{4,2},{5,3},{6,4},{7,5},{8,14},{9,15},{10,... | collective-permute-start | bytes 196616 | tf_op jit(solution)/shard_map/image_key_value_sum/ppermute | solution.py:34
  87.1 2.8 %collective-permute-done.12.refs_3_ = bf16[128,256]{1,0:T(8,128)(2,1)S(1)} collective-permute-done((bf16[128,256]{1,0:T(8,128)(2,1)S(1)}, bf16[128,256]{1,0:T(8,128)(2,1)S(1)}, u32[]{:S(2)}, u32[]{:S(2)}) %collective-permute-start.12) | collective-permute-done | bytes 65568 | tf_op jit(solution)/shard_map/image_key_value_sum/ppermute | solution.py:30
  90.7 10.1 %all-to-all-start.2 = ((bf16[32,16,128]{2,1,0:T(8,128)(2,1)}), bf16[32,16,128]{2,1,0:T(8,128)(2,1)S(1)}, u32[]{:S(2)}, u32[]{:S(2)}) async-start(bf16[32,16,128]{2,1,0:T(8,128)(2,1)} %bitcast.14), calls=%async_computation.3 | async-start | bytes 262144 | tf_op jit(solution)/shard_map/image_out_spread/all_to_all | solution.py:622
  101.0 8.7 %backward.2 = (f32[512,1024]{1,0:T(8,128)}, f32[4,128]{1,0:T(4,128)S(1)}, f32[8,128]{1,0:T(8,128)S(1)}) custom-call(s32[8]{0:T(128)S(1)} %iota.20.refs_0_, bf16[8192,128]{1,0:T(8,128)(2,1)} %all-gather.2.cloned.1.call-done.refs_1_, bf16[1024,1024]{1,0:T(8,128)(2,1)} %refs_6_.1, bf16[1024,1024]{1,0:T(8,128)(2,1)} %refs_7_.3, f32[1,1024]{1,0:T(1,128)S(1)} %bitcast.30, ...), custom_call_target="tpu_custom_call" | custom-call | flops 2147483648 | bytes 9443360 | tf_op jit(solution)/shard_map/backward/pallas_call | solution.py:61
  109.9 6.4 %backward.3 = (f32[256,1024]{1,0:T(8,128)}, f32[2,128]{1,0:T(2,128)S(1)}, f32[8,128]{1,0:T(8,128)}) custom-call(s32[8]{0:T(128)S(1)} %stack.35.refs_0_, bf16[1024,128]{1,0:T(8,128)(2,1)S(1)} %join.3.refs_1_, bf16[1024,128]{1,0:T(8,128)(2,1)S(1)} %collective-permute-done.15.refs_2_, bf16[1024,128]{1,0:T(8,128)(2,1)S(1)} %collective-permute-done.16.refs_3_, ...), custom_call_target="tpu_custom_call" | custom-call | flops 1073741824 | bytes 6820896 | tf_op jit(solution)/shard_map/backward/pallas_call | solution.py:61
  117.6 3.8 %collective-permute-start.21 = (f32[6,128]{1,0:T(8,128)S(1)}, f32[6,128]{1,0:T(8,128)S(1)}, u32[]{:S(2)}, u32[]{:S(2)}) collective-permute-start(f32[6,128]{1,0:T(8,128)S(1)} %fusion.5), channel_id=1, source_target_pairs={{0,6},{1,7},{2,0},{3,1},{4,2},{5,3},{6,4},{7,5},{8,14},{9,15},{10,... | collective-permute-start | bytes 9224 | tf_op jit(solution)/shard_map/inner_sum/ppermute | solution.py:34
  122.9 3.6 %collective-permute-done.22 = f32[6,128]{1,0:T(8,128)S(1)} collective-permute-done((f32[6,128]{1,0:T(8,128)S(1)}, f32[6,128]{1,0:T(8,128)S(1)}, u32[]{:S(2)}, u32[]{:S(2)}) %collective-permute-start.22) | collective-permute-done | bytes 3104 | tf_op jit(solution)/shard_map/inner_sum/ppermute | solution.py:38
  126.5 7.7 %image_backward.1 = (bf16[128,3200]{1,0:T(8,128)(2,1)}, f32[128,3200]{1,0:T(8,128)}, f32[8,128]{1,0:T(8,128)S(1)}) custom-call(s32[8]{0:T(128)S(1)} %fusion.2.refs_1_.refs_0_, f32[256,1024]{1,0:T(8,128)} %get-tuple-element.69.refs_1_, bf16[256,1024]{1,0:T(8,128)(2,1)S(1)} %copy-done, f32[2,128]{1,0:T(2,128)S(1)} %slice.31.refs_5_.refs_3_, ...), custom_call_target="tpu_custom_call" | custom-call | flops 1677721600 | bytes 10586144 | tf_op jit(solution)/shard_map/image_backward/pallas_call | solution.py:61
  134.3 2.4 %collective-permute-done.23 = bf16[128,3200]{1,0:T(8,128)(2,1)S(1)} collective-permute-done((bf16[128,3200]{1,0:T(8,128)(2,1)}, bf16[128,3200]{1,0:T(8,128)(2,1)S(1)}, u32[]{:S(2)}, u32[]{:S(2)}) %collective-permute-start.23) | collective-permute-done | bytes 819232 | tf_op jit(solution)/shard_map/d_vis_sum/ppermute | solution.py:42
  141.0 9.7 %all-to-all-start.3 = ((bf16[32,2,16,128]{3,2,1,0:T(8,128)(2,1)}), bf16[32,2,16,128]{3,2,1,0:T(8,128)(2,1)S(1)}, u32[]{:S(2)}, u32[]{:S(2)}) async-start(bf16[32,2,16,128]{3,2,1,0:T(8,128)(2,1)} %bitcast.19), calls=%async_computation.4 | async-start | bytes 524288 | tf_op jit(solution)/shard_map/image_out_collect/all_to_all | solution.py:639
  150.7 3.3 %collective-permute-start.25 = (bf16[32,3200]{1,0:T(8,128)(2,1)}, bf16[32,3200]{1,0:T(8,128)(2,1)S(1)}, u32[]{:S(2)}, u32[]{:S(2)}) collective-permute-start(bf16[32,3200]{1,0:T(8,128)(2,1)} %copy-done.11), channel_id=1, source_target_pairs={{0,6},{1,7},{2,0},{3,1},{4,2},{5,3},{6,4},{7,5},{8,14},{9,15},{10,... | collective-permute-start | bytes 614408 | tf_op jit(solution)/shard_map/d_vis_sum/ppermute | solution.py:34
  154.1 4.0 %collective-permute-done.25.refs_7_.refs_2_ = bf16[32,3200]{1,0:T(8,128)(2,1)S(1)} collective-permute-done((bf16[32,3200]{1,0:T(8,128)(2,1)}, bf16[32,3200]{1,0:T(8,128)(2,1)S(1)}, u32[]{:S(2)}, u32[]{:S(2)}) %collective-permute-start.25) | collective-permute-done | bytes 204832 | tf_op jit(solution)/shard_map/d_vis_sum/ppermute | solution.py:34
  158.1 3.7 %collective-permute-start.27 = (bf16[16,3200]{1,0:T(8,128)(2,1)S(1)}, bf16[16,3200]{1,0:T(8,128)(2,1)S(1)}, u32[]{:S(2)}, u32[]{:S(2)}) collective-permute-start(bf16[16,3200]{1,0:T(8,128)(2,1)S(1)} %add_convert_fusion), channel_id=1, source_target_pairs={{0,6},{1,7},{2,0},{3,1},{4,2},{5,3},{6,4},{7,5},{8,14},{9,15},{10,... | collective-permute-start | bytes 307208 | tf_op jit(solution)/shard_map/d_vis_sum/ppermute | solution.py:34
  162.0 3.9 %text_out.1 = (bf16[512,1024]{1,0:T(8,128)(2,1)}, f32[8,128]{1,0:T(8,128)}) custom-call(s32[2]{0:T(128)S(1)} %convert_element_type.27.refs_0_, f32[512,1024]{1,0:T(8,128)} %get-tuple-element.79.refs_1_, bf16[512,1024]{1,0:T(8,128)(2,1)S(1)} %copy-done.3, f32[4,128]{1,0:T(4,128)S(1)} %slice.28.refs_2_.refs_3_, f32[4,128]{1,0:T(4,128)S(1)} %slice.33.refs_4_, ...), custom_call_target="tpu_custom_call" | custom-call | bytes 4198408 | tf_op jit(solution)/shard_map/text_out/pallas_call | solution.py:61
  (112 shorter events, 28.6 us)
Async XLA Ops:
  7.2 93.7 %all-gather.2.cloned.1.call-start = ((), (), s32[]{:S(2)}) async-start(), calls=%async_computation.6 | async-start | bytes 2359296 | tf_op jit(solution)/shard_map/text_grad_gather/all_gather | solution.py:599
  13.3 13.3 %collective-permute-start.1 = (bf16[64,3200]{1,0:T(8,128)(2,1)S(1)}, bf16[64,3200]{1,0:T(8,128)(2,1)S(1)}, u32[]{:S(2)}, u32[]{:S(2)}) collective-permute-start(bf16[64,3200]{1,0:T(8,128)(2,1)S(1)} %join.2.refs_2_), channel_id=1, source_target_pairs={{0,2},{1,7},{2,4},{3,1},{4,6},{5,3},{6,0},{7,5},{8,10},{9,15},{10,... | collective-permute-start | bytes 1228808 | tf_op jit(solution)/shard_map/vision_gather/ppermute | solution.py:547
  15.0 22.9 %all-to-all-start = ((bf16[32,2,16,128]{3,2,1,0:T(8,128)(2,1)}), bf16[32,2,16,128]{3,2,1,0:T(8,128)(2,1)S(1)}, u32[]{:S(2)}, u32[]{:S(2)}) async-start(bf16[32,2,16,128]{3,2,1,0:T(8,128)(2,1)} %get-tuple-element.48), calls=%async_computation | async-start | bytes 524288 | tf_op jit(solution)/shard_map/slot_grads_spread/all_to_all | solution.py:597
  26.6 11.0 %collective-permute-start.3 = (bf16[32,3200]{1,0:T(8,128)(2,1)S(1)}, bf16[32,3200]{1,0:T(8,128)(2,1)S(1)}, u32[]{:S(2)}, u32[]{:S(2)}) collective-permute-start(bf16[32,3200]{1,0:T(8,128)(2,1)S(1)} %constant_dynamic-slice_fusion.1), channel_id=1, source_target_pairs={{0,2},{1,7},{2,4},{3,1},{4,6},{5,3},{6,0},{7,5},{8,10},{9,15},{10,... | collective-permute-start | bytes 614408 | tf_op jit(solution)/shard_map/vision_gather/ppermute | solution.py:548
  28.3 20.8 %collective-permute-start.2 = (bf16[64,3200]{1,0:T(8,128)(2,1)S(1)}, bf16[64,3200]{1,0:T(8,128)(2,1)S(1)}, u32[]{:S(2)}, u32[]{:S(2)}) collective-permute-start(bf16[64,3200]{1,0:T(8,128)(2,1)S(1)} %collective-permute-done.1.refs_3_), channel_id=1, source_target_pairs={{0,1},{1,0},{2,3},{3,2},{4,5},{5,4},{6,7},{7,6},{8,9},{9,8},{10,11... | collective-permute-start | bytes 1228808 | tf_op jit(solution)/shard_map/vision_gather/ppermute | solution.py:42
  37.7 11.4 %collective-permute-start.4 = (bf16[32,3200]{1,0:T(8,128)(2,1)S(1)}, bf16[32,3200]{1,0:T(8,128)(2,1)S(1)}, u32[]{:S(2)}, u32[]{:S(2)}) collective-permute-start(bf16[32,3200]{1,0:T(8,128)(2,1)S(1)} %collective-permute-done.3.refs_3_.refs_5_), channel_id=1, source_target_pairs={{0,1},{1,0},{2,3},{3,2},{4,5},{5,4},{6,7},{7,6},{8,9},{9,8},{10,11... | collective-permute-start | bytes 614408 | tf_op jit(solution)/shard_map/vision_gather/ppermute | solution.py:42
  39.1 19.9 %all-to-all-start.1 = ((bf16[32,16,128]{2,1,0:T(8,128)(2,1)}), bf16[32,16,128]{2,1,0:T(8,128)(2,1)S(1)}, u32[]{:S(2)}, u32[]{:S(2)}) async-start(bf16[32,16,128]{2,1,0:T(8,128)(2,1)} %get-tuple-element.58), calls=%async_computation.2 | async-start | bytes 262144 | tf_op jit(solution)/shard_map/slot_grads_collect/all_to_all | solution.py:604
  49.0 117.9 %reduce-scatter.2.cloned.1.call-start = ((), (), s32[]{:S(2)}) async-start(), calls=%async_computation.5 | async-start | bytes 2359296 | tf_op jit(solution)/shard_map/text_key_value_sum/reduce_scatter | solution.py:611
  58.9 8.8 %collective-permute-start.9 = (bf16[4,256,256]{2,1,0:T(8,128)(2,1)}, bf16[4,256,256]{2,1,0:T(8,128)(2,1)}, u32[]{:S(2)}, u32[]{:S(2)}) collective-permute-start(bf16[4,256,256]{2,1,0:T(8,128)(2,1)} %get-tuple-element.56), channel_id=1, source_target_pairs={{0,1},{1,0},{2,3},{3,2},{4,5},{5,4},{6,7},{7,6},{8,9},{9,8},{10,11... | collective-permute-start | bytes 1572872 | tf_op jit(solution)/shard_map/image_key_value_sum/ppermute | solution.py:42
  59.0 8.2 %collective-permute-start.14 = (bf16[512,128]{1,0:T(8,128)(2,1)S(1)}, bf16[512,128]{1,0:T(8,128)(2,1)S(1)}, u32[]{:S(2)}, u32[]{:S(2)}) collective-permute-start(bf16[512,128]{1,0:T(8,128)(2,1)S(1)} %bitcast.21), channel_id=1, source_target_pairs={{0,1},{1,0},{2,3},{3,2},{4,5},{5,4},{6,7},{7,6},{8,9},{9,8},{10,11... | collective-permute-start | bytes 393224 | tf_op jit(solution)/shard_map/image_grad_gather/ppermute | solution.py:42
  67.2 9.0 %collective-permute-start.15 = (bf16[1024,128]{1,0:T(8,128)(2,1)S(1)}, bf16[1024,128]{1,0:T(8,128)(2,1)S(1)}, u32[]{:S(2)}, u32[]{:S(2)}) collective-permute-start(bf16[1024,128]{1,0:T(8,128)(2,1)S(1)} %join.3.refs_1_), channel_id=1, source_target_pairs={{0,2},{1,7},{2,4},{3,1},{4,6},{5,3},{6,0},{7,5},{8,10},{9,15},{10,... | collective-permute-start | bytes 786440 | tf_op jit(solution)/shard_map/image_grad_gather/ppermute | solution.py:547
  69.5 8.3 %collective-permute-start.10 = (bf16[256,256]{1,0:T(8,128)(2,1)S(1)}, bf16[256,256]{1,0:T(8,128)(2,1)S(1)}, u32[]{:S(2)}, u32[]{:S(2)}) collective-permute-start(bf16[256,256]{1,0:T(8,128)(2,1)S(1)} %get-tuple-element.60), channel_id=1, source_target_pairs={{0,2},{1,3},{2,4},{3,5},{4,6},{5,7},{6,0},{7,1},{8,10},{9,11},{10,... | collective-permute-start | bytes 393224 | tf_op jit(solution)/shard_map/image_key_value_sum/ppermute | solution.py:30
  70.4 12.8 %collective-permute-start.7 = (f32[6,128]{1,0:T(8,128)S(1)}, f32[6,128]{1,0:T(8,128)S(1)}, u32[]{:S(2)}, u32[]{:S(2)}) collective-permute-start(f32[6,128]{1,0:T(8,128)S(1)} %fusion.6), channel_id=1, source_target_pairs={{0,6},{1,7},{2,0},{3,1},{4,2},{5,3},{6,4},{7,5},{8,14},{9,15},{10,... | collective-permute-start | bytes 9224 | tf_op jit(solution)/shard_map/squares_sum/ppermute | solution.py:34
  72.9 10.4 %collective-permute-start.8 = (f32[6,128]{1,0:T(8,128)S(1)}, f32[6,128]{1,0:T(8,128)S(1)}, u32[]{:S(2)}, u32[]{:S(2)}) collective-permute-start(f32[6,128]{1,0:T(8,128)S(1)} %fusion.6), channel_id=1, source_target_pairs={{0,4},{1,5},{2,6},{3,7},{4,0},{5,1},{6,2},{7,3},{8,12},{9,13},{10,... | collective-permute-start | bytes 9224 | tf_op jit(solution)/shard_map/squares_sum/ppermute | solution.py:38
  73.7 13.4 %collective-permute-start.6 = (f32[6,128]{1,0:T(8,128)S(1)}, f32[6,128]{1,0:T(8,128)S(1)}, u32[]{:S(2)}, u32[]{:S(2)}) collective-permute-start(f32[6,128]{1,0:T(8,128)S(1)} %fusion.6), channel_id=1, source_target_pairs={{0,2},{1,3},{2,4},{3,5},{4,6},{5,7},{6,0},{7,1},{8,10},{9,11},{10,... | collective-permute-start | bytes 9224 | tf_op jit(solution)/shard_map/squares_sum/ppermute | solution.py:30
  76.2 24.6 %collective-permute-start.17 = (bf16[512,128]{1,0:T(8,128)(2,1)S(1)}, bf16[512,128]{1,0:T(8,128)(2,1)S(1)}, u32[]{:S(2)}, u32[]{:S(2)}) collective-permute-start(bf16[512,128]{1,0:T(8,128)(2,1)S(1)} %constant_dynamic-slice_fusion), channel_id=1, source_target_pairs={{0,2},{1,7},{2,4},{3,1},{4,6},{5,3},{6,0},{7,5},{8,10},{9,15},{10,... | collective-permute-start | bytes 393224 | tf_op jit(solution)/shard_map/image_grad_gather/ppermute | solution.py:548
  83.3 26.4 %collective-permute-start.16 = (bf16[1024,128]{1,0:T(8,128)(2,1)S(1)}, bf16[1024,128]{1,0:T(8,128)(2,1)S(1)}, u32[]{:S(2)}, u32[]{:S(2)}) collective-permute-start(bf16[1024,128]{1,0:T(8,128)(2,1)S(1)} %collective-permute-done.15.refs_2_), channel_id=1, source_target_pairs={{0,1},{1,0},{2,3},{3,2},{4,5},{5,4},{6,7},{7,6},{8,9},{9,8},{10,11... | collective-permute-start | bytes 786440 | tf_op jit(solution)/shard_map/image_grad_gather/ppermute | solution.py:42
  90.7 19.2 %all-to-all-start.2 = ((bf16[32,16,128]{2,1,0:T(8,128)(2,1)}), bf16[32,16,128]{2,1,0:T(8,128)(2,1)S(1)}, u32[]{:S(2)}, u32[]{:S(2)}) async-start(bf16[32,16,128]{2,1,0:T(8,128)(2,1)} %bitcast.14), calls=%async_computation.3 | async-start | bytes 262144 | tf_op jit(solution)/shard_map/image_out_spread/all_to_all | solution.py:622
  100.8 8.9 %collective-permute-start.18 = (bf16[512,128]{1,0:T(8,128)(2,1)S(1)}, bf16[512,128]{1,0:T(8,128)(2,1)S(1)}, u32[]{:S(2)}, u32[]{:S(2)}) collective-permute-start(bf16[512,128]{1,0:T(8,128)(2,1)S(1)} %collective-permute-done.17.refs_4_), channel_id=1, source_target_pairs={{0,1},{1,0},{2,3},{3,2},{4,5},{5,4},{6,7},{7,6},{8,9},{9,8},{10,11... | collective-permute-start | bytes 393224 | tf_op jit(solution)/shard_map/image_grad_gather/ppermute | solution.py:42
  139.7 14.3 %collective-permute-start.24 = (bf16[32,3200]{1,0:T(8,128)(2,1)}, bf16[32,3200]{1,0:T(8,128)(2,1)S(1)}, u32[]{:S(2)}, u32[]{:S(2)}) collective-permute-start(bf16[32,3200]{1,0:T(8,128)(2,1)} %get-tuple-element.81), channel_id=1, source_target_pairs={{0,2},{1,3},{2,4},{3,5},{4,6},{5,7},{6,0},{7,1},{8,10},{9,11},{10,... | collective-permute-start | bytes 614408 | tf_op jit(solution)/shard_map/d_vis_sum/ppermute | solution.py:30
  141.0 25.9 %all-to-all-start.3 = ((bf16[32,2,16,128]{3,2,1,0:T(8,128)(2,1)}), bf16[32,2,16,128]{3,2,1,0:T(8,128)(2,1)S(1)}, u32[]{:S(2)}, u32[]{:S(2)}) async-start(bf16[32,2,16,128]{3,2,1,0:T(8,128)(2,1)} %bitcast.19), calls=%async_computation.4 | async-start | bytes 524288 | tf_op jit(solution)/shard_map/image_out_collect/all_to_all | solution.py:639
  150.7 7.4 %collective-permute-start.25 = (bf16[32,3200]{1,0:T(8,128)(2,1)}, bf16[32,3200]{1,0:T(8,128)(2,1)S(1)}, u32[]{:S(2)}, u32[]{:S(2)}) collective-permute-start(bf16[32,3200]{1,0:T(8,128)(2,1)} %copy-done.11), channel_id=1, source_target_pairs={{0,6},{1,7},{2,0},{3,1},{4,2},{5,3},{6,4},{7,5},{8,14},{9,15},{10,... | collective-permute-start | bytes 614408 | tf_op jit(solution)/shard_map/d_vis_sum/ppermute | solution.py:34
  154.0 11.9 %collective-permute-start.26 = (bf16[16,3200]{1,0:T(8,128)(2,1)S(1)}, bf16[16,3200]{1,0:T(8,128)(2,1)S(1)}, u32[]{:S(2)}, u32[]{:S(2)}) collective-permute-start(bf16[16,3200]{1,0:T(8,128)(2,1)S(1)} %add_convert_fusion.1), channel_id=1, source_target_pairs={{0,2},{1,3},{2,4},{3,5},{4,6},{5,7},{6,0},{7,1},{8,10},{9,11},{10,... | collective-permute-start | bytes 307208 | tf_op jit(solution)/shard_map/d_vis_sum/ppermute | solution.py:30
  158.1 7.8 %collective-permute-start.27 = (bf16[16,3200]{1,0:T(8,128)(2,1)S(1)}, bf16[16,3200]{1,0:T(8,128)(2,1)S(1)}, u32[]{:S(2)}, u32[]{:S(2)}) collective-permute-start(bf16[16,3200]{1,0:T(8,128)(2,1)S(1)} %add_convert_fusion), channel_id=1, source_target_pairs={{0,6},{1,7},{2,0},{3,1},{4,2},{5,3},{6,4},{7,5},{8,14},{9,15},{10,... | collective-permute-start | bytes 307208 | tf_op jit(solution)/shard_map/d_vis_sum/ppermute | solution.py:34
  (22 other events, 153.2 us)
Sparse Core Ops, SparseCore 0:
  11.8 31.7 all-gather.1
  67.9 37.2 reduce-scatter.1

commit v2 on v1

--- a/solution.py
+++ b/solution.py
@@ -623,22 +623,23 @@
             image_kv.reshape(dp, CHUNK, LANE), "dp", split_axis=0, concat_axis=0, tiled=True
         )
 
-    text_d, text_inner, text_back = backward(
-        rel, [text_g], w_key, w_value, gain, text_embed, [kv_ring, pieces[1], pieces[2]]
-    )
-    image_d, image_inner, _ = backward(where, image_g, w_key, w_value, gain, embed, [text_back, spread])
-    with jax.named_scope("inner_sum"):
-        inner = small_sum(jnp.concatenate([text_inner, image_inner]))
-    d_far, d_near, back_done = image_backward(
-        order, image_d, embed, image_square, inner[text_rows:], w_proj, [kv_out]
-    )
-    with jax.named_scope("d_vis_sum"):
-        d_pieces, d_ring = ring_sum(d_near.reshape(RING, -1, DV), d_far)
-    packed, _ = take_blocks(owner, spread, [d_ring])
+    packed, sent_done = take_blocks(owner, spread, ())
     with jax.named_scope("image_out_collect"):
         arrived = lax.all_to_all(
             packed.reshape(dp, slots, CHUNK, LANE), "dp", split_axis=0, concat_axis=0, tiled=True
         )
+
+    text_d, text_inner, text_back = backward(
+        rel, [text_g], w_key, w_value, gain, text_embed, [kv_ring, pieces[1], pieces[2]]
+    )
+    image_d, image_inner, _ = backward(where, image_g, w_key, w_value, gain, embed, [text_back, sent_done])
+    with jax.named_scope("inner_sum"):
+        inner = small_sum(jnp.concatenate([text_inner, image_inner]))
+    d_far, d_near, back_done = image_backward(
+        order, image_d, embed, image_square, inner[text_rows:], w_proj, [arrived]
+    )
+    with jax.named_scope("d_vis_sum"):
+        d_pieces, d_ring = ring_sum(d_near.reshape(RING, -1, DV), d_far)
     text_grad, _ = text_out(
         filled, text_d, text_embed, text_square, inner[:text_rows], [back_done, *d_pieces[1:3]]
     )

time: 177 us -> 177 us (level)
  waiting for transfers between devices: 31.3 us -> 40 us
  starting transfers between devices: 69.7 us -> 64.1 us
    ppermute x2, waiting for transfers between devices: 9.37 us -> 14.4 us  [chip_gather(): lax.ppermute(lax.dynamic_slice_in_dim(near, core[0] * rows, rows), 'mp',...]
    ppermute x6, starting transfers between devices: 18.6 us -> 15.1 us  [down(): return lax.ppermute(x, 'mp', DOWN)]
    ppermute x6, waiting for transfers between devices: 4.03 us -> 7.38 us  [up(): return lax.ppermute(x, 'mp', UP)]
    ppermute x2, starting transfers between devices: 1.74 us -> 4.26 us  [chip_gather(): near = lax.ppermute(block, 'mp', SPLIT)]
    ppermute x6, waiting for transfers between devices: 7.68 us -> 5.3 us  [down(): return lax.ppermute(x, 'mp', DOWN)]
    all_to_all x1, starting transfers between devices: 9.66 us -> 7.72 us  [shards(): lax.all_to_all(packed.reshape(dp, slots, CHUNK, LANE), 'dp', split_axis=0...]
    all_to_all x1, waiting for transfers between devices: 0.22 us -> 2.07 us  [shards(): lax.all_to_all(image_kv.reshape(dp, CHUNK, LANE), 'dp', split_axis=0, con...]
    unnamed x24 -> x22, local copies, waits for them, and re-layouts: 6.48 us -> 5.14 us
  transfers between devices with their start and end apart: 34 -> 34, of which waited for: 12 -> 15; matrix products, arithmetic and copies ran while one was open for 0% -> 0% of each run, Pallas kernels for 29% -> 28%
where the time goes in v2:
time: 177 us
  starting transfers between devices  64.1 us (36%)
  Pallas kernels  51.5 us (29%)
  waiting for transfers between devices  40 us (23%)
  between operations  14.5 us (8%)
  local copies, waits for them, and re-layouts  6.01 us (3%)
    pallas_call x17, Pallas kernels, call(): pl.pallas_call(body, in_specs=[SMEM if i < scalars else HBM if i in far e...  51.5 us
    ppermute x6, starting transfers between devices, down(): return lax.ppermute(x, 'mp', DOWN)  15.1 us
    ppermute x2, waiting for transfers between devices, chip_gather(): lax.ppermute(lax.dynamic_slice_in_dim(near, core[0] * rows, rows), 'mp',...  14.4 us
    all_to_all x1, starting transfers between devices, shards(): lax.all_to_all(grad_chunks, 'dp', split_axis=0, concat_axis=0, tiled=True)  11.6 us
    all_to_all x1, starting transfers between devices, shards(): lax.all_to_all(picked, 'dp', split_axis=0, concat_axis=0, tiled=True)  9.99 us
    all_to_all x1, starting transfers between devices, shards(): lax.all_to_all(image_kv.reshape(dp, CHUNK, LANE), 'dp', split_axis=0, con...  8.42 us
    all_to_all x1, starting transfers between devices, shards(): lax.all_to_all(packed.reshape(dp, slots, CHUNK, LANE), 'dp', split_axis=0...  7.72 us
    ppermute x6, waiting for transfers between devices, up(): return lax.ppermute(x, 'mp', UP)  7.38 us
  transfers between devices with their start and end apart: 34, of which 15 were waited for; matrix products, arithmetic and copies ran while one was open for 0% of the time, Pallas kernels for 28%

profile of v2, /device:TPU:2, one launch (start us, length us, event | category | flops | bytes accessed | tf_op | source)
XLA Modules:
  0.0 176.6 jit_solution(17754488914026505581)
XLA Ops:
  15.0 11.6 %all-to-all-start = ((bf16[32,2,16,128]{3,2,1,0:T(8,128)(2,1)}), bf16[32,2,16,128]{3,2,1,0:T(8,128)(2,1)S(1)}, u32[]{:S(2)}, u32[]{:S(2)}) async-start(bf16[32,2,16,128]{3,2,1,0:T(8,128)(2,1)} %get-tuple-element.47), calls=%async_computation | async-start | bytes 524288 | tf_op jit(solution)/shard_map/slot_grads_spread/all_to_all | solution.py:597
  28.3 9.4 %collective-permute-done.3.refs_3_.refs_5_ = bf16[32,3200]{1,0:T(8,128)(2,1)S(1)} collective-permute-done((bf16[32,3200]{1,0:T(8,128)(2,1)S(1)}, bf16[32,3200]{1,0:T(8,128)(2,1)S(1)}, u32[]{:S(2)}, u32[]{:S(2)}) %collective-permute-start.3) | collective-permute-done | bytes 204832 | tf_op jit(solution)/shard_map/vision_gather/ppermute | solution.py:548
  39.2 9.8 %image_forward.1 = (bf16[256,1024]{1,0:T(8,128)(2,1)}, bf16[4,256,256]{2,1,0:T(8,128)(2,1)}, f32[4,256,256]{2,1,0:T(8,128)}, f32[2,128]{1,0:T(2,128)S(1)}, f32[8,128]{1,0:T(8,128)S(1)}) custom-call(s32[8]{0:T(128)S(1)} %stack.35.refs_0_, s32[8]{0:T(128)S(1)} %fusion.2.refs_1_.refs_0_, bf16[64,3200]{1,0:T(8,128)(2,1)S(1)} %join.2.refs_2_, ...), custom_call_target="tpu_custom_call" | custom-call | flops 2751463424 | bytes 14488640 | tf_op jit(solution)/shard_map/image_forward/pallas_call | solution.py:61
  49.5 10.0 %all-to-all-start.1 = ((bf16[32,16,128]{2,1,0:T(8,128)(2,1)}), bf16[32,16,128]{2,1,0:T(8,128)(2,1)S(1)}, u32[]{:S(2)}, u32[]{:S(2)}) async-start(bf16[32,16,128]{2,1,0:T(8,128)(2,1)} %get-tuple-element.57), calls=%async_computation.2 | async-start | bytes 262144 | tf_op jit(solution)/shard_map/slot_grads_collect/all_to_all | solution.py:604
  59.5 7.7 %text_forward.1 = (bf16[8,512,256]{2,1,0:T(8,128)(2,1)}, f32[4,128]{1,0:T(4,128)S(1)}, f32[8,128]{1,0:T(8,128)S(1)}) custom-call(bf16[512,1024]{1,0:T(8,128)(2,1)S(1)} %copy-done.3, f32[1,1024]{1,0:T(1,128)S(1)} %bitcast.29, bf16[1024,1024]{1,0:T(8,128)(2,1)} %refs_6_.1, bf16[1024,1024]{1,0:T(8,128)(2,1)} %refs_7_.3, f32[8,128]{1,0:T(8,128)S(1)} %get-tuple-element.50.refs_4_), custom_call_target="tpu_custom_call" | custom-call | flops 2147483648 | bytes 7346176 | tf_op jit(solution)/shard_map/text_forward/pallas_call | solution.py:61
  69.0 3.3 %collective-permute-start.7 = (f32[6,128]{1,0:T(8,128)S(1)}, f32[6,128]{1,0:T(8,128)S(1)}, u32[]{:S(2)}, u32[]{:S(2)}) collective-permute-start(f32[6,128]{1,0:T(8,128)S(1)} %fusion.6), channel_id=1, source_target_pairs={{0,6},{1,7},{2,0},{3,1},{4,2},{5,3},{6,4},{7,5},{8,14},{9,15},{10,... | collective-permute-start | bytes 9224 | tf_op jit(solution)/shard_map/squares_sum/ppermute | solution.py:34
  73.3 2.6 %collective-permute-start.15 = (bf16[1024,128]{1,0:T(8,128)(2,1)S(1)}, bf16[1024,128]{1,0:T(8,128)(2,1)S(1)}, u32[]{:S(2)}, u32[]{:S(2)}) collective-permute-start(bf16[1024,128]{1,0:T(8,128)(2,1)S(1)} %join.3.refs_1_), channel_id=1, source_target_pairs={{0,2},{1,7},{2,4},{3,1},{4,6},{5,3},{6,0},{7,5},{8,10},{9,15},{10,... | collective-permute-start | bytes 786440 | tf_op jit(solution)/shard_map/image_grad_gather/ppermute | solution.py:547
  76.7 5.1 %collective-permute-done.11.refs_2_.refs_8_ = bf16[256,256]{1,0:T(8,128)(2,1)S(1)} collective-permute-done((bf16[256,256]{1,0:T(8,128)(2,1)S(1)}, bf16[256,256]{1,0:T(8,128)(2,1)S(1)}, u32[]{:S(2)}, u32[]{:S(2)}) %collective-permute-start.11) | collective-permute-done | bytes 131104 | tf_op jit(solution)/shard_map/image_key_value_sum/ppermute | solution.py:34
  82.5 2.6 %collective-permute-start.13 = (bf16[128,256]{1,0:T(8,128)(2,1)S(1)}, bf16[128,256]{1,0:T(8,128)(2,1)S(1)}, u32[]{:S(2)}, u32[]{:S(2)}) collective-permute-start(bf16[128,256]{1,0:T(8,128)(2,1)S(1)} %add_convert_fusion.2), channel_id=1, source_target_pairs={{0,6},{1,7},{2,0},{3,1},{4,2},{5,3},{6,4},{7,5},{8,14},{9,15},{10,... | collective-permute-start | bytes 196616 | tf_op jit(solution)/shard_map/image_key_value_sum/ppermute | solution.py:34
  85.1 2.1 %collective-permute-done.12.refs_3_ = bf16[128,256]{1,0:T(8,128)(2,1)S(1)} collective-permute-done((bf16[128,256]{1,0:T(8,128)(2,1)S(1)}, bf16[128,256]{1,0:T(8,128)(2,1)S(1)}, u32[]{:S(2)}, u32[]{:S(2)}) %collective-permute-start.12) | collective-permute-done | bytes 65568 | tf_op jit(solution)/shard_map/image_key_value_sum/ppermute | solution.py:30
  88.1 8.4 %all-to-all-start.2 = ((bf16[32,16,128]{2,1,0:T(8,128)(2,1)}), bf16[32,16,128]{2,1,0:T(8,128)(2,1)S(1)}, u32[]{:S(2)}, u32[]{:S(2)}) async-start(bf16[32,16,128]{2,1,0:T(8,128)(2,1)} %bitcast.14), calls=%async_computation.3 | async-start | bytes 262144 | tf_op jit(solution)/shard_map/image_out_spread/all_to_all | solution.py:622
  98.7 5.0 %collective-permute-done.17.refs_4_ = bf16[512,128]{1,0:T(8,128)(2,1)S(1)} collective-permute-done((bf16[512,128]{1,0:T(8,128)(2,1)S(1)}, bf16[512,128]{1,0:T(8,128)(2,1)S(1)}, u32[]{:S(2)}, u32[]{:S(2)}) %collective-permute-start.17) | collective-permute-done | bytes 131104 | tf_op jit(solution)/shard_map/image_grad_gather/ppermute | solution.py:548
  103.7 2.1 %all-to-all-done.2.refs_1_ = bf16[32,16,128]{2,1,0:T(8,128)(2,1)S(1)} async-done(((bf16[32,16,128]{2,1,0:T(8,128)(2,1)}), bf16[32,16,128]{2,1,0:T(8,128)(2,1)S(1)}, u32[]{:S(2)}, u32[]{:S(2)}) %all-to-all-start.2) | async-done | bytes 131104 | tf_op jit(solution)/shard_map/image_out_spread/all_to_all | solution.py:622
  107.0 7.7 %all-to-all-start.3 = ((bf16[32,2,16,128]{3,2,1,0:T(8,128)(2,1)}), bf16[32,2,16,128]{3,2,1,0:T(8,128)(2,1)S(1)}, u32[]{:S(2)}, u32[]{:S(2)}) async-start(bf16[32,2,16,128]{3,2,1,0:T(8,128)(2,1)} %bitcast.15), calls=%async_computation.4 | async-start | bytes 524288 | tf_op jit(solution)/shard_map/image_out_collect/all_to_all | solution.py:628
  114.8 8.6 %backward.2 = (f32[512,1024]{1,0:T(8,128)}, f32[4,128]{1,0:T(4,128)S(1)}, f32[8,128]{1,0:T(8,128)S(1)}) custom-call(s32[8]{0:T(128)S(1)} %iota.20.refs_0_, bf16[8192,128]{1,0:T(8,128)(2,1)} %all-gather.2.cloned.1.call-done.refs_1_, bf16[1024,1024]{1,0:T(8,128)(2,1)} %refs_6_.1, bf16[1024,1024]{1,0:T(8,128)(2,1)} %refs_7_.3, f32[1,1024]{1,0:T(1,128)S(1)} %bitcast.30, ...), custom_call_target="tpu_custom_call" | custom-call | flops 2147483648 | bytes 9443360 | tf_op jit(solution)/shard_map/backward/pallas_call | solution.py:61
  123.5 6.4 %backward.3 = (f32[256,1024]{1,0:T(8,128)}, f32[2,128]{1,0:T(2,128)S(1)}, f32[8,128]{1,0:T(8,128)}) custom-call(s32[8]{0:T(128)S(1)} %stack.35.refs_0_, bf16[1024,128]{1,0:T(8,128)(2,1)S(1)} %join.3.refs_1_, bf16[1024,128]{1,0:T(8,128)(2,1)S(1)} %collective-permute-done.15.refs_2_, bf16[1024,128]{1,0:T(8,128)(2,1)S(1)} %collective-permute-done.16.refs_3_, ...), custom_call_target="tpu_custom_call" | custom-call | flops 1073741824 | bytes 6820896 | tf_op jit(solution)/shard_map/backward/pallas_call | solution.py:61
  131.2 2.2 %collective-permute-start.21 = (f32[6,128]{1,0:T(8,128)S(1)}, f32[6,128]{1,0:T(8,128)S(1)}, u32[]{:S(2)}, u32[]{:S(2)}) collective-permute-start(f32[6,128]{1,0:T(8,128)S(1)} %fusion.5), channel_id=1, source_target_pairs={{0,6},{1,7},{2,0},{3,1},{4,2},{5,3},{6,4},{7,5},{8,14},{9,15},{10,... | collective-permute-start | bytes 9224 | tf_op jit(solution)/shard_map/inner_sum/ppermute | solution.py:34
  134.9 3.6 %collective-permute-done.22 = f32[6,128]{1,0:T(8,128)S(1)} collective-permute-done((f32[6,128]{1,0:T(8,128)S(1)}, f32[6,128]{1,0:T(8,128)S(1)}, u32[]{:S(2)}, u32[]{:S(2)}) %collective-permute-start.22) | collective-permute-done | bytes 3104 | tf_op jit(solution)/shard_map/inner_sum/ppermute | solution.py:38
  138.5 7.4 %image_backward.1 = (bf16[128,3200]{1,0:T(8,128)(2,1)S(1)}, f32[128,3200]{1,0:T(8,128)}, f32[8,128]{1,0:T(8,128)S(1)}) custom-call(s32[8]{0:T(128)S(1)} %fusion.2.refs_1_.refs_0_, f32[256,1024]{1,0:T(8,128)} %get-tuple-element.75.refs_1_, bf16[256,1024]{1,0:T(8,128)(2,1)S(1)} %copy-done, f32[2,128]{1,0:T(2,128)S(1)} %slice.31.refs_5_.refs_3_, ...), custom_call_target="tpu_custom_call" | custom-call | flops 1677721600 | bytes 10586144 | tf_op jit(solution)/shard_map/image_backward/pallas_call | solution.py:61
  145.9 2.3 %collective-permute-done.23 = bf16[128,3200]{1,0:T(8,128)(2,1)S(1)} collective-permute-done((bf16[128,3200]{1,0:T(8,128)(2,1)S(1)}, bf16[128,3200]{1,0:T(8,128)(2,1)S(1)}, u32[]{:S(2)}, u32[]{:S(2)}) %collective-permute-start.23) | collective-permute-done | bytes 819232 | tf_op jit(solution)/shard_map/d_vis_sum/ppermute | solution.py:42
  150.4 3.2 %collective-permute-start.25 = (bf16[32,3200]{1,0:T(8,128)(2,1)S(1)}, bf16[32,3200]{1,0:T(8,128)(2,1)S(1)}, u32[]{:S(2)}, u32[]{:S(2)}) collective-permute-start(bf16[32,3200]{1,0:T(8,128)(2,1)S(1)} %get-tuple-element.80), channel_id=1, source_target_pairs={{0,6},{1,7},{2,0},{3,1},{4,2},{5,3},{6,4},{7,5},{8,14},{9,15},{10,... | collective-permute-start | bytes 614408 | tf_op jit(solution)/shard_map/d_vis_sum/ppermute | solution.py:34
  153.6 5.1 %collective-permute-done.24.refs_6_.refs_1_ = bf16[32,3200]{1,0:T(8,128)(2,1)S(1)} collective-permute-done((bf16[32,3200]{1,0:T(8,128)(2,1)S(1)}, bf16[32,3200]{1,0:T(8,128)(2,1)S(1)}, u32[]{:S(2)}, u32[]{:S(2)}) %collective-permute-start.24) | collective-permute-done | bytes 204832 | tf_op jit(solution)/shard_map/d_vis_sum/ppermute | solution.py:30
  158.9 3.3 %collective-permute-start.27 = (bf16[16,3200]{1,0:T(8,128)(2,1)S(1)}, bf16[16,3200]{1,0:T(8,128)(2,1)S(1)}, u32[]{:S(2)}, u32[]{:S(2)}) collective-permute-start(bf16[16,3200]{1,0:T(8,128)(2,1)S(1)} %add_convert_fusion), channel_id=1, source_target_pairs={{0,6},{1,7},{2,0},{3,1},{4,2},{5,3},{6,4},{7,5},{8,14},{9,15},{10,... | collective-permute-start | bytes 307208 | tf_op jit(solution)/shard_map/d_vis_sum/ppermute | solution.py:34
  162.4 3.9 %text_out.1 = (bf16[512,1024]{1,0:T(8,128)(2,1)}, f32[8,128]{1,0:T(8,128)}) custom-call(s32[2]{0:T(128)S(1)} %convert_element_type.27.refs_0_, f32[512,1024]{1,0:T(8,128)} %get-tuple-element.69.refs_1_, bf16[512,1024]{1,0:T(8,128)(2,1)S(1)} %copy-done.3, f32[4,128]{1,0:T(4,128)S(1)} %slice.28.refs_2_.refs_3_, f32[4,128]{1,0:T(4,128)S(1)} %slice.32.refs_4_, ...), custom_call_target="tpu_custom_call" | custom-call | bytes 4198408 | tf_op jit(solution)/shard_map/text_out/pallas_call | solution.py:61
  (110 shorter events, 28.7 us)
Async XLA Ops:
  7.2 107.6 %all-gather.2.cloned.1.call-start = ((), (), s32[]{:S(2)}) async-start(), calls=%async_computation.6 | async-start | bytes 2359296 | tf_op jit(solution)/shard_map/text_grad_gather/all_gather | solution.py:599
  13.3 13.3 %collective-permute-start.1 = (bf16[64,3200]{1,0:T(8,128)(2,1)S(1)}, bf16[64,3200]{1,0:T(8,128)(2,1)S(1)}, u32[]{:S(2)}, u32[]{:S(2)}) collective-permute-start(bf16[64,3200]{1,0:T(8,128)(2,1)S(1)} %join.2.refs_2_), channel_id=1, source_target_pairs={{0,2},{1,7},{2,4},{3,1},{4,6},{5,3},{6,0},{7,5},{8,10},{9,15},{10,... | collective-permute-start | bytes 1228808 | tf_op jit(solution)/shard_map/vision_gather/ppermute | solution.py:547
  15.0 22.9 %all-to-all-start = ((bf16[32,2,16,128]{3,2,1,0:T(8,128)(2,1)}), bf16[32,2,16,128]{3,2,1,0:T(8,128)(2,1)S(1)}, u32[]{:S(2)}, u32[]{:S(2)}) async-start(bf16[32,2,16,128]{3,2,1,0:T(8,128)(2,1)} %get-tuple-element.47), calls=%async_computation | async-start | bytes 524288 | tf_op jit(solution)/shard_map/slot_grads_spread/all_to_all | solution.py:597
  26.7 11.0 %collective-permute-start.3 = (bf16[32,3200]{1,0:T(8,128)(2,1)S(1)}, bf16[32,3200]{1,0:T(8,128)(2,1)S(1)}, u32[]{:S(2)}, u32[]{:S(2)}) collective-permute-start(bf16[32,3200]{1,0:T(8,128)(2,1)S(1)} %constant_dynamic-slice_fusion.1), channel_id=1, source_target_pairs={{0,2},{1,7},{2,4},{3,1},{4,6},{5,3},{6,0},{7,5},{8,10},{9,15},{10,... | collective-permute-start | bytes 614408 | tf_op jit(solution)/shard_map/vision_gather/ppermute | solution.py:548
  28.3 10.8 %collective-permute-start.2 = (bf16[64,3200]{1,0:T(8,128)(2,1)S(1)}, bf16[64,3200]{1,0:T(8,128)(2,1)S(1)}, u32[]{:S(2)}, u32[]{:S(2)}) collective-permute-start(bf16[64,3200]{1,0:T(8,128)(2,1)S(1)} %collective-permute-done.1.refs_3_), channel_id=1, source_target_pairs={{0,1},{1,0},{2,3},{3,2},{4,5},{5,4},{6,7},{7,6},{8,9},{9,8},{10,11... | collective-permute-start | bytes 1228808 | tf_op jit(solution)/shard_map/vision_gather/ppermute | solution.py:42
  49.1 19.8 %collective-permute-start.9 = (bf16[4,256,256]{2,1,0:T(8,128)(2,1)}, bf16[4,256,256]{2,1,0:T(8,128)(2,1)S(1)}, u32[]{:S(2)}, u32[]{:S(2)}) collective-permute-start(bf16[4,256,256]{2,1,0:T(8,128)(2,1)} %get-tuple-element.55), channel_id=1, source_target_pairs={{0,1},{1,0},{2,3},{3,2},{4,5},{5,4},{6,7},{7,6},{8,9},{9,8},{10,11... | collective-permute-start | bytes 1572872 | tf_op jit(solution)/shard_map/image_key_value_sum/ppermute | solution.py:42
  49.5 19.3 %all-to-all-start.1 = ((bf16[32,16,128]{2,1,0:T(8,128)(2,1)}), bf16[32,16,128]{2,1,0:T(8,128)(2,1)S(1)}, u32[]{:S(2)}, u32[]{:S(2)}) async-start(bf16[32,16,128]{2,1,0:T(8,128)(2,1)} %get-tuple-element.57), calls=%async_computation.2 | async-start | bytes 262144 | tf_op jit(solution)/shard_map/slot_grads_collect/all_to_all | solution.py:604
  68.9 7.2 %collective-permute-start.10 = (bf16[256,256]{1,0:T(8,128)(2,1)S(1)}, bf16[256,256]{1,0:T(8,128)(2,1)S(1)}, u32[]{:S(2)}, u32[]{:S(2)}) collective-permute-start(bf16[256,256]{1,0:T(8,128)(2,1)S(1)} %get-tuple-element.59), channel_id=1, source_target_pairs={{0,2},{1,3},{2,4},{3,5},{4,6},{5,7},{6,0},{7,1},{8,10},{9,11},{10,... | collective-permute-start | bytes 393224 | tf_op jit(solution)/shard_map/image_key_value_sum/ppermute | solution.py:30
  69.0 13.5 %collective-permute-start.7 = (f32[6,128]{1,0:T(8,128)S(1)}, f32[6,128]{1,0:T(8,128)S(1)}, u32[]{:S(2)}, u32[]{:S(2)}) collective-permute-start(f32[6,128]{1,0:T(8,128)S(1)} %fusion.6), channel_id=1, source_target_pairs={{0,6},{1,7},{2,0},{3,1},{4,2},{5,3},{6,4},{7,5},{8,14},{9,15},{10,... | collective-permute-start | bytes 9224 | tf_op jit(solution)/shard_map/squares_sum/ppermute | solution.py:34
  72.3 12.8 %collective-permute-start.8 = (f32[6,128]{1,0:T(8,128)S(1)}, f32[6,128]{1,0:T(8,128)S(1)}, u32[]{:S(2)}, u32[]{:S(2)}) collective-permute-start(f32[6,128]{1,0:T(8,128)S(1)} %fusion.6), channel_id=1, source_target_pairs={{0,4},{1,5},{2,6},{3,7},{4,0},{5,1},{6,2},{7,3},{8,12},{9,13},{10,... | collective-permute-start | bytes 9224 | tf_op jit(solution)/shard_map/squares_sum/ppermute | solution.py:38
  72.7 12.4 %collective-permute-start.6 = (f32[6,128]{1,0:T(8,128)S(1)}, f32[6,128]{1,0:T(8,128)S(1)}, u32[]{:S(2)}, u32[]{:S(2)}) collective-permute-start(f32[6,128]{1,0:T(8,128)S(1)} %fusion.6), channel_id=1, source_target_pairs={{0,2},{1,3},{2,4},{3,5},{4,6},{5,7},{6,0},{7,1},{8,10},{9,11},{10,... | collective-permute-start | bytes 9224 | tf_op jit(solution)/shard_map/squares_sum/ppermute | solution.py:30
  73.3 24.0 %collective-permute-start.15 = (bf16[1024,128]{1,0:T(8,128)(2,1)S(1)}, bf16[1024,128]{1,0:T(8,128)(2,1)S(1)}, u32[]{:S(2)}, u32[]{:S(2)}) collective-permute-start(bf16[1024,128]{1,0:T(8,128)(2,1)S(1)} %join.3.refs_1_), channel_id=1, source_target_pairs={{0,2},{1,7},{2,4},{3,1},{4,6},{5,3},{6,0},{7,5},{8,10},{9,15},{10,... | collective-permute-start | bytes 786440 | tf_op jit(solution)/shard_map/image_grad_gather/ppermute | solution.py:547
  76.1 5.7 %collective-permute-start.11 = (bf16[256,256]{1,0:T(8,128)(2,1)S(1)}, bf16[256,256]{1,0:T(8,128)(2,1)S(1)}, u32[]{:S(2)}, u32[]{:S(2)}) collective-permute-start(bf16[256,256]{1,0:T(8,128)(2,1)S(1)} %get-tuple-element.60), channel_id=1, source_target_pairs={{0,6},{1,7},{2,0},{3,1},{4,2},{5,3},{6,4},{7,5},{8,14},{9,15},{10,... | collective-permute-start | bytes 393224 | tf_op jit(solution)/shard_map/image_key_value_sum/ppermute | solution.py:34
  81.8 5.5 %collective-permute-start.12 = (bf16[128,256]{1,0:T(8,128)(2,1)S(1)}, bf16[128,256]{1,0:T(8,128)(2,1)S(1)}, u32[]{:S(2)}, u32[]{:S(2)}) collective-permute-start(bf16[128,256]{1,0:T(8,128)(2,1)S(1)} %add_convert_fusion.3), channel_id=1, source_target_pairs={{0,2},{1,3},{2,4},{3,5},{4,6},{5,7},{6,0},{7,1},{8,10},{9,11},{10,... | collective-permute-start | bytes 196616 | tf_op jit(solution)/shard_map/image_key_value_sum/ppermute | solution.py:30
  88.1 17.7 %all-to-all-start.2 = ((bf16[32,16,128]{2,1,0:T(8,128)(2,1)}), bf16[32,16,128]{2,1,0:T(8,128)(2,1)S(1)}, u32[]{:S(2)}, u32[]{:S(2)}) async-start(bf16[32,16,128]{2,1,0:T(8,128)(2,1)} %bitcast.14), calls=%async_computation.3 | async-start | bytes 262144 | tf_op jit(solution)/shard_map/image_out_spread/all_to_all | solution.py:622
  96.5 70.8 %reduce-scatter.2.cloned.1.call-start = ((), (), s32[]{:S(2)}) async-start(), calls=%async_computation.5 | async-start | bytes 2359296 | tf_op jit(solution)/shard_map/text_key_value_sum/reduce_scatter | solution.py:611
  97.3 6.4 %collective-permute-start.17 = (bf16[512,128]{1,0:T(8,128)(2,1)S(1)}, bf16[512,128]{1,0:T(8,128)(2,1)S(1)}, u32[]{:S(2)}, u32[]{:S(2)}) collective-permute-start(bf16[512,128]{1,0:T(8,128)(2,1)S(1)} %constant_dynamic-slice_fusion), channel_id=1, source_target_pairs={{0,2},{1,7},{2,4},{3,1},{4,6},{5,3},{6,0},{7,5},{8,10},{9,15},{10,... | collective-permute-start | bytes 393224 | tf_op jit(solution)/shard_map/image_grad_gather/ppermute | solution.py:548
  98.6 24.9 %collective-permute-start.16 = (bf16[1024,128]{1,0:T(8,128)(2,1)S(1)}, bf16[1024,128]{1,0:T(8,128)(2,1)S(1)}, u32[]{:S(2)}, u32[]{:S(2)}) collective-permute-start(bf16[1024,128]{1,0:T(8,128)(2,1)S(1)} %collective-permute-done.15.refs_2_), channel_id=1, source_target_pairs={{0,1},{1,0},{2,3},{3,2},{4,5},{5,4},{6,7},{7,6},{8,9},{9,8},{10,11... | collective-permute-start | bytes 786440 | tf_op jit(solution)/shard_map/image_grad_gather/ppermute | solution.py:42
  103.7 19.8 %collective-permute-start.18 = (bf16[512,128]{1,0:T(8,128)(2,1)S(1)}, bf16[512,128]{1,0:T(8,128)(2,1)S(1)}, u32[]{:S(2)}, u32[]{:S(2)}) collective-permute-start(bf16[512,128]{1,0:T(8,128)(2,1)S(1)} %collective-permute-done.17.refs_4_), channel_id=1, source_target_pairs={{0,1},{1,0},{2,3},{3,2},{4,5},{5,4},{6,7},{7,6},{8,9},{9,8},{10,11... | collective-permute-start | bytes 393224 | tf_op jit(solution)/shard_map/image_grad_gather/ppermute | solution.py:42
  107.0 31.4 %all-to-all-start.3 = ((bf16[32,2,16,128]{3,2,1,0:T(8,128)(2,1)}), bf16[32,2,16,128]{3,2,1,0:T(8,128)(2,1)S(1)}, u32[]{:S(2)}, u32[]{:S(2)}) async-start(bf16[32,2,16,128]{3,2,1,0:T(8,128)(2,1)} %bitcast.15), calls=%async_computation.4 | async-start | bytes 524288 | tf_op jit(solution)/shard_map/image_out_collect/all_to_all | solution.py:628
  150.4 8.3 %collective-permute-start.24 = (bf16[32,3200]{1,0:T(8,128)(2,1)S(1)}, bf16[32,3200]{1,0:T(8,128)(2,1)S(1)}, u32[]{:S(2)}, u32[]{:S(2)}) collective-permute-start(bf16[32,3200]{1,0:T(8,128)(2,1)S(1)} %get-tuple-element.79), channel_id=1, source_target_pairs={{0,2},{1,3},{2,4},{3,5},{4,6},{5,7},{6,0},{7,1},{8,10},{9,11},{10,... | collective-permute-start | bytes 614408 | tf_op jit(solution)/shard_map/d_vis_sum/ppermute | solution.py:30
  150.4 8.5 %collective-permute-start.25 = (bf16[32,3200]{1,0:T(8,128)(2,1)S(1)}, bf16[32,3200]{1,0:T(8,128)(2,1)S(1)}, u32[]{:S(2)}, u32[]{:S(2)}) collective-permute-start(bf16[32,3200]{1,0:T(8,128)(2,1)S(1)} %get-tuple-element.80), channel_id=1, source_target_pairs={{0,6},{1,7},{2,0},{3,1},{4,2},{5,3},{6,4},{7,5},{8,14},{9,15},{10,... | collective-permute-start | bytes 614408 | tf_op jit(solution)/shard_map/d_vis_sum/ppermute | solution.py:34
  158.8 7.5 %collective-permute-start.26 = (bf16[16,3200]{1,0:T(8,128)(2,1)S(1)}, bf16[16,3200]{1,0:T(8,128)(2,1)S(1)}, u32[]{:S(2)}, u32[]{:S(2)}) collective-permute-start(bf16[16,3200]{1,0:T(8,128)(2,1)S(1)} %add_convert_fusion.1), channel_id=1, source_target_pairs={{0,2},{1,3},{2,4},{3,5},{4,6},{5,7},{6,0},{7,1},{8,10},{9,11},{10,... | collective-permute-start | bytes 307208 | tf_op jit(solution)/shard_map/d_vis_sum/ppermute | solution.py:30
  158.9 7.4 %collective-permute-start.27 = (bf16[16,3200]{1,0:T(8,128)(2,1)S(1)}, bf16[16,3200]{1,0:T(8,128)(2,1)S(1)}, u32[]{:S(2)}, u32[]{:S(2)}) collective-permute-start(bf16[16,3200]{1,0:T(8,128)(2,1)S(1)} %add_convert_fusion), channel_id=1, source_target_pairs={{0,6},{1,7},{2,0},{3,1},{4,2},{5,3},{6,4},{7,5},{8,14},{9,15},{10,... | collective-permute-start | bytes 307208 | tf_op jit(solution)/shard_map/d_vis_sum/ppermute | solution.py:34
  (21 other events, 145.2 us)
Sparse Core Ops, SparseCore 0:
  11.9 31.7 all-gather.1
  99.9 37.8 reduce-scatter.1
